TPU v7x, 128 devices: a whole 4x4x4 slice. The times are simulated.
128 devices in a mesh: node: 16 (over y, x), local: 8 (over z, core).
Axes of the slice: x: 4, y: 4, z: 4, core: 2. Of those that a mesh axis runs over, the one named last changes fastest.
Arguments:
- tokens: bfloat16 [2048, 3584], P(('node', 'local')), may hold values from -6 to 6
- upstream: bfloat16 [2048, 3584], P(('node', 'local')), may hold values from -6 to 6
- routes: int32 [2048, 8], P(('node', 'local')), may hold values from 0 to 47, as said below
- combine: float32 [2048, 8], P(('node', 'local')), may hold values from 0.05 to 0.3
- seq_ids: int32 [2048], P(('node', 'local')), may hold values from 0 to 255, never falling along the last dimension, each value on 1 to 16 neighbouring positions
- ratios: float32 [256], replicated, may hold values from 0.25 to 4
- w_gate: bfloat16 [48, 3584, 1024], P('node', None, 'local'), may hold values from -0.09375 to 0.09375
- w_up: bfloat16 [48, 3584, 1024], P('node', None, 'local'), may hold values from -0.09375 to 0.09375
- w_down: bfloat16 [48, 1024, 3584], P('node', 'local'), may hold values from -0.1875 to 0.1875
Outputs:
- grad_tokens: bfloat16 [2048, 3584], P(('node', 'local'))
- grad_combine: float32 [2048, 8], P(('node', 'local'))
- grad_gate: bfloat16 [48, 3584, 1024], P('node', None, 'local')
- grad_up: bfloat16 [48, 3584, 1024], P('node', None, 'local')
- grad_down: bfloat16 [48, 1024, 3584], P('node', 'local')
Inputs may be any that keep to these rules, and one draw needn't show every extreme that they name: `routes`: each row names 8 distinct experts, two in each of 4 distinct node groups. The rows of one device fall into classes of 5 rows (the last class smaller) whose rows name the same node groups; different classes of a device name disjoint groups, so no node group is named by more than 5 rows of one device, and in every draw each device has a group named by exactly 5 of its rows.
All inputs are finite; a program needn't handle non-finite values.
Results may differ from a plain program's by a relative error of at most 0.015.
Values may be sent and summed in bfloat16 or wider, within the bound.
A program may use at most 192 MiB of HBM per device.

v0:
```python
import jax
import jax.numpy as jnp
from jax import lax
from jax.sharding import PartitionSpec as P


def local(tokens, upstream, routes, combine, seq_ids, ratios, w_gate, w_up, w_down):
    node_count = lax.axis_size("node")
    local_count = lax.axis_size("local")
    tok_rows = tokens.shape[0]
    features = tokens.shape[1]
    per_group = w_gate.shape[0]
    top_count = routes.shape[1]
    capacity = 5 * tok_rows // node_count
    clipped = jnp.minimum(ratios, 1.0)
    seq_hot = seq_ids[:, None] == jnp.arange(ratios.shape[0], dtype=jnp.int32)[None, :]
    seq_weight = jnp.sum(jnp.where(seq_hot, clipped[None, :], 0.0), axis=1)
    route_weight = (combine * seq_weight[:, None]).astype(jnp.bfloat16)
    expert_hot = (
        routes[:, :, None] == jnp.arange(node_count * per_group, dtype=jnp.int32)[None, None, :]
    )
    expert_weight = jnp.sum(
        jnp.where(expert_hot, route_weight.astype(jnp.float32)[:, :, None], 0.0), axis=1
    )
    expert_weight = expert_weight.reshape(tok_rows, node_count, per_group)
    group_hit = jnp.any(expert_hot.reshape(tok_rows, top_count, node_count, per_group), axis=(1, 3))
    slot_index = jnp.cumsum(group_hit.astype(jnp.int32), axis=0) - 1
    placing = group_hit[:, :, None] & (
        slot_index[:, :, None] == jnp.arange(capacity, dtype=jnp.int32)[None, None, :]
    )
    place_mask = placing.astype(jnp.bfloat16)
    send_tokens = jnp.einsum(
        "tgc,td->gcd", place_mask, tokens, preferred_element_type=jnp.float32
    ).astype(jnp.bfloat16)
    send_upstream = jnp.einsum(
        "tgc,td->gcd", place_mask, upstream, preferred_element_type=jnp.float32
    ).astype(jnp.bfloat16)
    send_weight = jnp.einsum(
        "tgc,tge->gce", placing.astype(jnp.float32), expert_weight, precision=lax.Precision.HIGHEST
    ).astype(jnp.bfloat16)

    def spread(source_array):
        shape_tail = source_array.shape[1:]
        widened = jnp.broadcast_to(source_array[:, None], (node_count, local_count) + shape_tail)
        return widened.reshape((node_count * local_count,) + shape_tail)

    arrived = (
        lax.all_to_all(
            spread(send_tokens), ("node", "local"), split_axis=0, concat_axis=0, tiled=True
        ),
        lax.all_to_all(
            spread(send_upstream), ("node", "local"), split_axis=0, concat_axis=0, tiled=True
        ),
        lax.all_to_all(
            spread(send_weight), ("node", "local"), split_axis=0, concat_axis=0, tiled=True
        ),
    )
    in_rows = arrived[0].reshape(-1, features)
    in_upstream = arrived[1].reshape(-1, features)
    route_scale = arrived[2].reshape(-1, per_group).astype(jnp.float32)
    partial_value = jnp.zeros((in_rows.shape[0], features), jnp.float32)
    score_list = []
    grad_gate = []
    grad_up = []
    grad_down = []
    contract_last = (((1,), (1,)), ((), ()))
    contract_first = (((0,), (0,)), ((), ()))
    for expert in range(per_group):
        gate_pre = jnp.dot(in_rows, w_gate[expert], preferred_element_type=jnp.float32)
        up_pre = jnp.dot(in_rows, w_up[expert], preferred_element_type=jnp.float32)
        projected = lax.dot_general(
            in_upstream, w_down[expert], contract_last, preferred_element_type=jnp.float32
        )
        gate_sigmoid = jax.nn.sigmoid(gate_pre)
        activated = gate_pre * gate_sigmoid
        hidden = (activated * up_pre).astype(jnp.bfloat16)
        score_list.append(jnp.sum(hidden.astype(jnp.float32) * projected, axis=1))
        row_scale = route_scale[:, expert : expert + 1]
        d_hidden = row_scale * projected
        d_gate = (
            d_hidden * up_pre * gate_sigmoid * (1.0 + gate_pre * (1.0 - gate_sigmoid))
        ).astype(jnp.bfloat16)
        d_up = (d_hidden * activated).astype(jnp.bfloat16)
        scaled = (hidden.astype(jnp.float32) * row_scale).astype(jnp.bfloat16)
        partial_value = partial_value + lax.dot_general(
            d_gate, w_gate[expert], contract_last, preferred_element_type=jnp.float32
        )
        partial_value = partial_value + lax.dot_general(
            d_up, w_up[expert], contract_last, preferred_element_type=jnp.float32
        )
        grad_gate.append(
            lax.dot_general(
                in_rows, d_gate, contract_first, preferred_element_type=jnp.float32
            ).astype(jnp.bfloat16)
        )
        grad_up.append(
            lax.dot_general(
                in_rows, d_up, contract_first, preferred_element_type=jnp.float32
            ).astype(jnp.bfloat16)
        )
        grad_down.append(
            lax.dot_general(
                scaled, in_upstream, contract_first, preferred_element_type=jnp.float32
            ).astype(jnp.bfloat16)
        )
    score_block = jnp.stack(score_list, axis=1)
    returned = (
        lax.all_to_all(
            partial_value.astype(jnp.bfloat16).reshape(
                node_count * local_count, capacity, features
            ),
            ("node", "local"),
            split_axis=0,
            concat_axis=0,
            tiled=True,
        ),
        lax.all_to_all(
            score_block.astype(jnp.bfloat16).reshape(node_count * local_count, capacity, per_group),
            ("node", "local"),
            split_axis=0,
            concat_axis=0,
            tiled=True,
        ),
    )
    group_grad = jnp.sum(
        returned[0].astype(jnp.float32).reshape(node_count, local_count, capacity, features), axis=1
    ).astype(jnp.bfloat16)
    group_score = jnp.sum(
        returned[1].astype(jnp.float32).reshape(node_count, local_count, capacity, per_group),
        axis=1,
    ).astype(jnp.bfloat16)
    grad_tokens = jnp.einsum(
        "tgc,gcd->td", place_mask, group_grad, preferred_element_type=jnp.float32
    ).astype(jnp.bfloat16)
    token_score = jnp.einsum(
        "tgc,gce->tge",
        placing.astype(jnp.float32),
        group_score.astype(jnp.float32),
        precision=lax.Precision.HIGHEST,
    ).reshape(tok_rows, node_count * per_group)
    grad_combine = seq_weight[:, None] * jnp.sum(
        jnp.where(expert_hot, token_score[:, None, :], 0.0), axis=2
    )
    return (
        grad_tokens,
        grad_combine,
        jnp.stack(grad_gate),
        jnp.stack(grad_up),
        jnp.stack(grad_down),
    )


def solution(mesh):
    return jax.shard_map(
        local,
        mesh=mesh,
        in_specs=(
            P(("node", "local"), None),
            P(("node", "local"), None),
            P(("node", "local"), None),
            P(("node", "local"), None),
            P(("node", "local")),
            P(),
            P("node", None, "local"),
            P("node", None, "local"),
            P("node", "local", None),
        ),
        out_specs=(
            P(("node", "local"), None),
            P(("node", "local"), None),
            P("node", None, "local"),
            P("node", None, "local"),
            P("node", "local", None),
        ),
        check_vma=False,
    )
```

profile of v0, /device:TPU:1, one launch (start us, length us, event | category | flops | bytes accessed | tf_op | source)
XLA Modules:
  0.0 433.8 jit_solution(1846669029910421066)
XLA Ops:
  3.5 3.5 broadcast_in_dim.71
  6.9 11.9 %all-to-all-start.2 = ((bf16[128,5,3584]{2,1,0:T(8,128)(2,1)}), bf16[128,5,3584]{2,1,0:T(8,128)(2,1)}, u32[]{:S(2)}, u32[]{:S(2)}) async-start(bf16[128,5,3584]{2,1,0:T(8,128)(2,1)} %bitcast.126), calls=%async_computation.2 | async-start | bytes 14680064 | tf_op jit(solution)/shard_map/all_to_all | solution.py:48
  19.5 89.1 %all-to-all-done.2 = bf16[128,5,3584]{2,1,0:T(8,128)(2,1)} async-done(((bf16[128,5,3584]{2,1,0:T(8,128)(2,1)}), bf16[128,5,3584]{2,1,0:T(8,128)(2,1)}, u32[]{:S(2)}, u32[]{:S(2)}) %all-to-all-start.2) | async-done | bytes 4587552 | tf_op jit(solution)/shard_map/all_to_all | solution.py:48
  108.6 3.5 broadcast_in_dim.70
  112.1 7.9 %all-to-all-start.1 = ((bf16[128,5,3584]{2,1,0:T(8,128)(2,1)}), bf16[128,5,3584]{2,1,0:T(8,128)(2,1)}, u32[]{:S(2)}, u32[]{:S(2)}) async-start(bf16[128,5,3584]{2,1,0:T(8,128)(2,1)} %bitcast.125), calls=%async_computation.1 | async-start | bytes 14680064 | tf_op jit(solution)/shard_map/all_to_all | solution.py:51
  121.5 8.2 %reshape.82 = bf16[640,3584]{1,0:T(8,128)(2,1)} reshape(bf16[128,5,3584]{2,1,0:T(8,128)(2,1)} %all-to-all-done.2) | data formatting | bytes 9175040 | tf_op jit(solution)/shard_map/reshape | solution.py:58
  129.7 3.9 fusion.12
  133.7 1.5 fusion.21
  135.5 2.2 fusion.15
  137.7 2.2 fusion.25
  139.9 2.2 fusion.31
  142.2 2.2 fusion.35
  144.4 64.9 %all-to-all-done.1 = bf16[128,5,3584]{2,1,0:T(8,128)(2,1)} async-done(((bf16[128,5,3584]{2,1,0:T(8,128)(2,1)}), bf16[128,5,3584]{2,1,0:T(8,128)(2,1)}, u32[]{:S(2)}, u32[]{:S(2)}) %all-to-all-start.1) | async-done | bytes 4587552 | tf_op jit(solution)/shard_map/all_to_all | solution.py:51
  209.3 8.1 %reshape.80 = bf16[640,3584]{1,0:T(8,128)(2,1)} reshape(bf16[128,5,3584]{2,1,0:T(8,128)(2,1)} %all-to-all-done.1) | data formatting | bytes 9175040 | tf_op jit(solution)/shard_map/reshape | solution.py:59
  217.4 5.0 %fusion.55 = (bf16[640]{0:T(1024)(128)(2,1)S(1)}, bf16[640,128]{0,1:T(8,128)(2,1)}, f32[640,128]{0,1:T(8,128)}) fusion(f32[640,128]{0,1:T(8,128)} %fusion.35, f32[640,128]{0,1:T(8,128)} %fusion.31, bf16[640,3584]{1,0:T(8,128)(2,1)} %reshape.80, bf16[3,128,3584]{2,1,0:T(8,128)(2,1)} %param.17), kind=kOutput, calls=%fused_computation.80 | convolution fusion | flops 587939200 | bytes 6653184 | tf_op jit(solution)/shard_map/dot_general | solution.py:71
  222.6 4.8 %fusion.57 = (bf16[640]{0:T(1024)(128)(2,1)S(1)}, bf16[640,128]{0,1:T(8,128)(2,1)}, f32[640,128]{0,1:T(8,128)}) fusion(f32[640,128]{0,1:T(8,128)} %fusion.25, f32[640,128]{0,1:T(8,128)S(1)} %fusion.21, bf16[640,3584]{1,0:T(8,128)(2,1)} %reshape.80, bf16[3,128,3584]{2,1,0:T(8,128)(2,1)} %param.17), kind=kOutput, calls=%fused_computation.82 | convolution fusion | flops 587939200 | bytes 6653184 | tf_op jit(solution)/shard_map/dot_general | solution.py:71
  228.3 4.9 %fusion.59 = (bf16[640]{0:T(1024)(128)(2,1)S(1)}, bf16[640,128]{0,1:T(8,128)(2,1)}, f32[640,128]{0,1:T(8,128)}) fusion(f32[640,128]{0,1:T(8,128)} %fusion.15, f32[640,128]{0,1:T(8,128)S(1)} %fusion.12, bf16[640,3584]{1,0:T(8,128)(2,1)} %reshape.80, bf16[3,128,3584]{2,1,0:T(8,128)(2,1)} %param.17), kind=kOutput, calls=%fused_computation.84 | convolution fusion | flops 587939200 | bytes 6653184 | tf_op jit(solution)/shard_map/dot_general | solution.py:71
  235.5 11.0 %all-to-all-start.4 = ((bf16[128,5,3]{1,2,0:T(4,128)(2,1)}), bf16[128,5,3]{1,2,0:T(4,128)(2,1)}, u32[]{:S(2)}, u32[]{:S(2)}) async-start(bf16[128,5,3]{1,2,0:T(4,128)(2,1)} %copy.89), calls=%async_computation.4 | async-start | bytes 262144 | tf_op jit(solution)/shard_map/all_to_all | solution.py:117
  247.3 8.9 %all-to-all-done.4 = bf16[128,5,3]{1,2,0:T(4,128)(2,1)} async-done(((bf16[128,5,3]{1,2,0:T(4,128)(2,1)}), bf16[128,5,3]{1,2,0:T(4,128)(2,1)}, u32[]{:S(2)}, u32[]{:S(2)}) %all-to-all-start.4) | async-done | bytes 3872 | tf_op jit(solution)/shard_map/all_to_all | solution.py:117
  256.2 1.0 bitcast_reduce_fusion.1
  259.9 5.4 %all-to-all-start = ((bf16[128,5,3]{1,2,0:T(4,128)(2,1)}), bf16[128,5,3]{1,2,0:T(4,128)(2,1)}, u32[]{:S(2)}, u32[]{:S(2)}) async-start(bf16[128,5,3]{1,2,0:T(4,128)(2,1)} %bitcast.127), calls=%async_computation | async-start | bytes 262144 | tf_op jit(solution)/shard_map/all_to_all | solution.py:54
  266.7 8.5 %all-to-all-done = bf16[128,5,3]{1,2,0:T(4,128)(2,1)} async-done(((bf16[128,5,3]{1,2,0:T(4,128)(2,1)}), bf16[128,5,3]{1,2,0:T(4,128)(2,1)}, u32[]{:S(2)}, u32[]{:S(2)}) %all-to-all-start) | async-done | bytes 3872 | tf_op jit(solution)/shard_map/all_to_all | solution.py:54
  275.2 1.0 copy.81
  277.0 1.1 reshape.88
  278.2 1.3 multiply_convert_fusion.7
  279.6 4.9 %fusion.29 = f32[640,3584]{1,0:T(8,128)} fusion(bf16[640,128]{0,1:T(8,128)(2,1)S(1)} %get-tuple-element.29, bf16[3,3584,128]{2,1,0:T(8,128)(2,1)S(1)} %copy-done.3), kind=kOutput, calls=%fused_computation.48 | convolution fusion | flops 587202560 | bytes 10256384 | tf_op jit(solution)/shard_map/dot_general | solution.py:85
  284.6 5.0 %fusion.33 = f32[640,3584]{1,0:T(8,128)} fusion(bf16[640,128]{0,1:T(8,128)(2,1)S(1)} %get-tuple-element.28, bf16[3,3584,128]{2,1,0:T(8,128)(2,1)S(1)} %copy-done.5), kind=kOutput, calls=%fused_computation.52 | convolution fusion | flops 587202560 | bytes 10256384 | tf_op jit(solution)/shard_map/dot_general | solution.py:88
  289.5 1.0 multiply_convert_fusion.3
  290.6 4.9 %fusion.19 = f32[640,3584]{1,0:T(8,128)} fusion(bf16[640,128]{0,1:T(8,128)(2,1)S(1)} %get-tuple-element.36, bf16[3,3584,128]{2,1,0:T(8,128)(2,1)S(1)} %copy-done.3), kind=kOutput, calls=%fused_computation.38 | convolution fusion | flops 587202560 | bytes 10256384 | tf_op jit(solution)/shard_map/dot_general | solution.py:85
  295.4 4.9 %fusion.23 = f32[640,3584]{1,0:T(8,128)} fusion(bf16[640,128]{0,1:T(8,128)(2,1)S(1)} %get-tuple-element.35, bf16[3,3584,128]{2,1,0:T(8,128)(2,1)S(1)} %copy-done.5), kind=kOutput, calls=%fused_computation.42 | convolution fusion | flops 587202560 | bytes 10256384 | tf_op jit(solution)/shard_map/dot_general | solution.py:88
  300.3 5.0 %fusion.10 = f32[640,3584]{1,0:T(8,128)} fusion(bf16[640,128]{0,1:T(8,128)(2,1)S(1)} %get-tuple-element.27, bf16[3,3584,128]{2,1,0:T(8,128)(2,1)S(1)} %copy-done.3), kind=kOutput, calls=%fused_computation.29 | convolution fusion | flops 587202560 | bytes 10256384 | tf_op jit(solution)/shard_map/dot_general | solution.py:85
  305.4 19.2 %add_convert_fusion = bf16[640,3584]{1,0:T(8,128)(2,1)} fusion(f32[640,3584]{1,0:T(8,128)} %fusion.10, f32[640,3584]{1,0:T(8,128)} %fusion.23, f32[640,3584]{1,0:T(8,128)} %fusion.19, f32[640,3584]{1,0:T(8,128)} %fusion.29, f32[640,3584]{1,0:T(8,128)} %fusion.33, bf16[640,128]{0,1:T(8,128)(2,1)S(1)} %copy-done.18, bf16[3,3584,128]{2,1,0:T(8,128)(2,1)} %param.16), kind=kOutput, calls=%fused_computation | convolution fusion | flops 600965120 | bytes 51544064 | tf_op jit(solution)/shard_map/dot_general | solution.py:88
  324.5 7.9 %reshape.83 = bf16[128,5,3584]{2,1,0:T(8,128)(2,1)} reshape(bf16[640,3584]{1,0:T(8,128)(2,1)} %add_convert_fusion) | data formatting | bytes 9175040 | tf_op jit(solution)/shard_map/reshape | solution.py:109
  332.4 5.9 %all-to-all-start.3 = ((bf16[128,5,3584]{2,1,0:T(8,128)(2,1)}), bf16[128,5,3584]{2,1,0:T(8,128)(2,1)}, u32[]{:S(2)}, u32[]{:S(2)}) async-start(bf16[128,5,3584]{2,1,0:T(8,128)(2,1)} %reshape.83), calls=%async_computation.3 | async-start | bytes 14680064 | tf_op jit(solution)/shard_map/all_to_all | solution.py:108
  338.4 3.3 fusion.6
  341.7 3.2 fusion.8
  345.0 3.2 fusion.7
  348.2 1.5 fusion.5
  349.7 1.5 fusion.2
  351.2 1.5 fusion.4
  352.7 1.5 fusion.1
  354.2 1.5 fusion.3
  355.7 1.5 fusion
  357.2 1.8 pad_maximum_fusion.2
  359.0 1.8 pad_maximum_fusion
  360.8 1.8 pad_maximum_fusion.1
  362.7 65.4 %all-to-all-done.3 = bf16[128,5,3584]{2,1,0:T(8,128)(2,1)} async-done(((bf16[128,5,3584]{2,1,0:T(8,128)(2,1)}), bf16[128,5,3584]{2,1,0:T(8,128)(2,1)}, u32[]{:S(2)}, u32[]{:S(2)}) %all-to-all-start.3) | async-done | bytes 4587552 | tf_op jit(solution)/shard_map/all_to_all | solution.py:108
  428.0 4.6 %bitcast_reduce_fusion = bf16[16,5,3584]{2,1,0:T(8,128)(2,1)S(1)} fusion(bf16[128,5,3584]{2,1,0:T(8,128)(2,1)} %all-to-all-done.3), kind=kLoop, calls=%fused_computation.1 | loop fusion | flops 2007040 | bytes 5160960 | tf_op jit(solution)/shard_map/reduce_sum | solution.py:125
  (111 shorter events, 15.4 us)
Async XLA Ops:
  0.6 2.1 copy-start
  1.5 0.6 copy-start.27
  1.7 5.3 %copy-start.31 = (pred[16,16]{0,1:T(8,128)(4,1)}, pred[16,16]{0,1:T(8,128)(4,1)S(1)}, u32[]{:S(2)}) copy-start(pred[16,16]{0,1:T(8,128)(4,1)S(1)} %copy.76) | copy-start | bytes 772
  2.0 0.6 copy-start.29
  2.8 16.1 %copy-start.25 = (pred[16,16,5]{1,0,2:T(8,128)(4,1)}, pred[16,16,5]{1,0,2:T(8,128)(4,1)S(1)}, u32[]{:S(2)}) copy-start(pred[16,16,5]{1,0,2:T(8,128)(4,1)S(1)} %copy.87) | copy-start | bytes 3844
  6.9 11.9 %copy-start.24 = (bf16[16,3584]{1,0:T(8,128)(2,1)S(1)}, bf16[16,3584]{1,0:T(8,128)(2,1)}, u32[]{:S(2)}) copy-start(bf16[16,3584]{1,0:T(8,128)(2,1)} %param.10) | copy-start | bytes 344068
  6.9 101.7 %all-to-all-start.2 = ((bf16[128,5,3584]{2,1,0:T(8,128)(2,1)}), bf16[128,5,3584]{2,1,0:T(8,128)(2,1)}, u32[]{:S(2)}, u32[]{:S(2)}) async-start(bf16[128,5,3584]{2,1,0:T(8,128)(2,1)} %bitcast.126), calls=%async_computation.2 | async-start | bytes 14680064 | tf_op jit(solution)/shard_map/all_to_all | solution.py:48
  112.1 8.0 %copy-start.32 = (f32[16,8]{0,1:T(8,128)S(1)}, f32[16,8]{0,1:T(8,128)}, u32[]{:S(2)}) copy-start(f32[16,8]{0,1:T(8,128)} %param.12) | copy-start | bytes 1540
  112.1 8.6 %copy-start.33 = (f32[256]{0:T(256)S(1)}, f32[256]{0:T(256)}, u32[]{:S(2)}) copy-start(f32[256]{0:T(256)} %param.14) | copy-start | bytes 3076
  112.1 8.7 %copy-start.34 = (s32[16]{0:T(128)S(1)}, s32[16]{0:T(128)}, u32[]{:S(2)}) copy-start(s32[16]{0:T(128)} %param.13) | copy-start | bytes 196
  112.1 97.2 %all-to-all-start.1 = ((bf16[128,5,3584]{2,1,0:T(8,128)(2,1)}), bf16[128,5,3584]{2,1,0:T(8,128)(2,1)}, u32[]{:S(2)}, u32[]{:S(2)}) async-start(bf16[128,5,3584]{2,1,0:T(8,128)(2,1)} %bitcast.125), calls=%async_computation.1 | async-start | bytes 14680064 | tf_op jit(solution)/shard_map/all_to_all | solution.py:51
  121.5 8.3 %copy-start.3 = (bf16[3,3584,128]{2,1,0:T(8,128)(2,1)S(1)}, bf16[3,3584,128]{2,1,0:T(8,128)(2,1)}, u32[]{:S(2)}) copy-start(bf16[3,3584,128]{2,1,0:T(8,128)(2,1)} %param.15) | copy-start | bytes 8257540
  129.7 4.0 copy-start.2
  133.7 1.8 copy-start.4
  228.3 28.9 %copy-start.30 = (s32[16,16]{0,1:T(8,128)S(1)}, s32[16,16]{0,1:T(8,128)}, u32[]{:S(2)}) copy-start(s32[16,16]{0,1:T(8,128)} %copy-done.29) | copy-start | bytes 3076
  228.3 29.8 %copy-start.28 = (s32[16,8]{1,0:T(8,128)S(1)}, s32[16,8]{1,0:T(8,128)}, u32[]{:S(2)}) copy-start(s32[16,8]{1,0:T(8,128)} %copy-done.27) | copy-start | bytes 1540
  235.5 20.7 %all-to-all-start.4 = ((bf16[128,5,3]{1,2,0:T(4,128)(2,1)}), bf16[128,5,3]{1,2,0:T(4,128)(2,1)}, u32[]{:S(2)}, u32[]{:S(2)}) async-start(bf16[128,5,3]{1,2,0:T(4,128)(2,1)} %copy.89), calls=%async_computation.4 | async-start | bytes 262144 | tf_op jit(solution)/shard_map/all_to_all | solution.py:117
  259.9 15.2 %all-to-all-start = ((bf16[128,5,3]{1,2,0:T(4,128)(2,1)}), bf16[128,5,3]{1,2,0:T(4,128)(2,1)}, u32[]{:S(2)}, u32[]{:S(2)}) async-start(bf16[128,5,3]{1,2,0:T(4,128)(2,1)} %bitcast.127), calls=%async_computation | async-start | bytes 262144 | tf_op jit(solution)/shard_map/all_to_all | solution.py:54
  279.6 5.0 %copy-start.14 = (bf16[640,128]{0,1:T(8,128)(2,1)}, bf16[640,128]{0,1:T(8,128)(2,1)S(1)}, u32[]{:S(2)}) copy-start(bf16[640,128]{0,1:T(8,128)(2,1)S(1)} %get-tuple-element.29) | copy-start | bytes 491524
  279.6 5.0 %copy-start.16 = (bf16[640,128]{0,1:T(8,128)(2,1)}, bf16[640,128]{0,1:T(8,128)(2,1)S(1)}, u32[]{:S(2)}) copy-start(bf16[640,128]{0,1:T(8,128)(2,1)S(1)} %get-tuple-element.28) | copy-start | bytes 491524
  279.6 5.0 %copy-start.5 = (bf16[3,3584,128]{2,1,0:T(8,128)(2,1)S(1)}, bf16[3,3584,128]{2,1,0:T(8,128)(2,1)}, u32[]{:S(2)}) copy-start(bf16[3,3584,128]{2,1,0:T(8,128)(2,1)} %param.16) | copy-start | bytes 8257540
  284.5 5.0 %copy-start.6 = (f32[640,128]{0,1:T(8,128)S(1)}, f32[640,128]{0,1:T(8,128)}, u32[]{:S(2)}) copy-start(f32[640,128]{0,1:T(8,128)} %fusion.15) | copy-start | bytes 983044
  284.5 5.0 %copy-start.7 = (f32[640,128]{0,1:T(8,128)S(1)}, f32[640,128]{0,1:T(8,128)}, u32[]{:S(2)}) copy-start(f32[640,128]{0,1:T(8,128)} %fusion.25) | copy-start | bytes 983044
  284.6 5.0 %copy-start.19 = (f32[640,128]{0,1:T(8,128)S(1)}, f32[640,128]{0,1:T(8,128)}, u32[]{:S(2)}) copy-start(f32[640,128]{0,1:T(8,128)} %get-tuple-element.33) | copy-start | bytes 983044
  284.6 5.0 %copy-start.20 = (f32[640,128]{0,1:T(8,128)S(1)}, f32[640,128]{0,1:T(8,128)}, u32[]{:S(2)}) copy-start(f32[640,128]{0,1:T(8,128)} %get-tuple-element.32) | copy-start | bytes 983044
  290.6 4.9 %copy-start.8 = (bf16[640,128]{0,1:T(8,128)(2,1)}, bf16[640,128]{0,1:T(8,128)(2,1)S(1)}, u32[]{:S(2)}) copy-start(bf16[640,128]{0,1:T(8,128)(2,1)S(1)} %get-tuple-element.36) | copy-start | bytes 491524
  290.6 4.9 %copy-start.10 = (bf16[640,128]{0,1:T(8,128)(2,1)}, bf16[640,128]{0,1:T(8,128)(2,1)S(1)}, u32[]{:S(2)}) copy-start(bf16[640,128]{0,1:T(8,128)(2,1)S(1)} %get-tuple-element.35) | copy-start | bytes 491524
  290.6 9.8 %copy-start.12 = (bf16[640,128]{0,1:T(8,128)(2,1)}, bf16[640,128]{0,1:T(8,128)(2,1)S(1)}, u32[]{:S(2)}) copy-start(bf16[640,128]{0,1:T(8,128)(2,1)S(1)} %get-tuple-element.27) | copy-start | bytes 491524
  300.3 5.0 %copy-start.18 = (bf16[640,128]{0,1:T(8,128)(2,1)S(1)}, bf16[640,128]{0,1:T(8,128)(2,1)}, u32[]{:S(2)}) copy-start(bf16[640,128]{0,1:T(8,128)(2,1)} %get-tuple-element.26) | copy-start | bytes 491524
  332.4 5.9 %copy-start.22 = (bf16[640,128]{0,1:T(8,128)(2,1)S(1)}, bf16[640,128]{0,1:T(8,128)(2,1)}, u32[]{:S(2)}) copy-start(bf16[640,128]{0,1:T(8,128)(2,1)} %get-tuple-element.21) | copy-start | bytes 491524
  332.4 95.6 %all-to-all-start.3 = ((bf16[128,5,3584]{2,1,0:T(8,128)(2,1)}), bf16[128,5,3584]{2,1,0:T(8,128)(2,1)}, u32[]{:S(2)}, u32[]{:S(2)}) async-start(bf16[128,5,3584]{2,1,0:T(8,128)(2,1)} %reshape.83), calls=%async_computation.3 | async-start | bytes 14680064 | tf_op jit(solution)/shard_map/all_to_all | solution.py:108
  338.3 3.4 copy-start.23
  338.3 6.6 %copy-start.21 = (bf16[640,128]{0,1:T(8,128)(2,1)S(1)}, bf16[640,128]{0,1:T(8,128)(2,1)}, u32[]{:S(2)}) copy-start(bf16[640,128]{0,1:T(8,128)(2,1)} %get-tuple-element.23) | copy-start | bytes 491524
  338.4 9.8 %slice-start = ((s8[4587520]{0:T(1024)(128)(4,1)}), s8[4194304]{0:T(1024)(128)(4,1)S(1)}, s32[]{:S(2)}) async-start(s8[4587520]{0:T(1024)(128)(4,1)} %bitcast.123), calls=%async_computation.5 | async-start | bytes 8388608
  341.7 6.5 %slice-start.1 = ((s8[4587520]{0:T(1024)(128)(4,1)}), s8[393216]{0:T(1024)(128)(4,1)S(1)}, s32[]{:S(2)}) async-start(s8[4587520]{0:T(1024)(128)(4,1)} %bitcast.123), calls=%async_computation.6 | async-start | bytes 786432
  348.2 1.5 copy-start.13
  349.7 1.5 copy-start.11
  351.2 1.5 copy-start.9
  352.7 1.5 copy-start.17
  354.2 1.5 copy-start.15
  360.8 72.7 %copy-start.1 = (bf16[16,3584]{1,0:T(8,128)(2,1)S(1)}, bf16[16,3584]{1,0:T(8,128)(2,1)}, u32[]{:S(2)}) copy-start(bf16[16,3584]{1,0:T(8,128)(2,1)} %param.9) | copy-start | bytes 344068
  362.7 69.9 %copy-start.26 = (pred[16,16,5]{1,0,2:T(8,128)(4,1)S(1)}, pred[16,16,5]{1,0,2:T(8,128)(4,1)}, u32[]{:S(2)}) copy-start(pred[16,16,5]{1,0,2:T(8,128)(4,1)} %copy-done.25) | copy-start | bytes 3844
where the time goes:
time: 438 us; the launch traced here: 434 us
  waiting for transfers between devices  237 us (54%)
  matrix products  94.8 us (22%)
  starting transfers between devices  42.1 us (10%)
  local copies, waits for them, and re-layouts  42 us (10%)
  other arithmetic  16.7 us (4%)
    all_to_all x1, waiting for transfers between devices, local(): lax.all_to_all(spread(send_tokens), ('node', 'local'), split_axis=0, conc...  89.1 us
    all_to_all x1, waiting for transfers between devices, local(): lax.all_to_all(partial_value.astype(jnp.bfloat16).reshape(node_count * lo...  65.4 us
    all_to_all x1, waiting for transfers between devices, local(): lax.all_to_all(spread(send_upstream), ('node', 'local'), split_axis=0, co...  64.9 us
    dot_general x3, matrix products, local(): lax.dot_general(d_up, w_up[expert], contract_last, preferred_element_type...  29 us
    dot_general x3, matrix products, local(): lax.dot_general(d_gate, w_gate[expert], contract_last, preferred_element_...  14.8 us
    dot_general x3, matrix products, local(): lax.dot_general(in_upstream, w_down[expert], contract_last, preferred_ele...  14.7 us
    all_to_all x1, starting transfers between devices, local(): lax.all_to_all(spread(send_tokens), ('node', 'local'), split_axis=0, conc...  11.9 us
    all_to_all x1, starting transfers between devices, local(): lax.all_to_all(score_block.astype(jnp.bfloat16).reshape(node_count * loca...  11 us
  transfers between devices with their start and end apart: 5, of which 5 were waited for; matrix products, arithmetic and copies ran while one was open for 12% of the time, Pallas kernels for 0%

commit v1 on v0

v1 whole, which is shorter than its diff:
```python
import jax
import jax.numpy as jnp
from jax import lax
from jax.experimental import pallas as pl
from jax.experimental.pallas import tpu as pltpu
from jax.sharding import PartitionSpec as P

MESH = pl.DeviceIdType.MESH
BF = jnp.bfloat16
F32 = jnp.float32
I32 = jnp.int32

D = 3584
DT = D + 128
PW = 1152
ROWS = 80
CA = 1792
POS = {0: 0, 1: 1, 3: 2, 2: 3}
NT = (((1,), (1,)), ((), ()))
TN = (((0,), (0,)), ((), ()))


def slot(dz, dc):
    return pl.ds((POS[dz] * 2 + dc) * ROWS, ROWS)


def inverse(q):
    return ((-(q // 4)) % 4) * 4 + (-(q % 4)) % 4


def iota(shape, dim):
    return lax.broadcasted_iota(I32, shape, dim)


def one_hot(mask):
    return jnp.where(mask, 1.0, 0.0).astype(BF)


def kernel(
    tok, ups, routes, routes_t, combine, seq_ids, ratios, wg, wu, wd,
    gt, gc, gg, gu, gd,
    amat, bmat, x3, pack_t, pack_u, pack_b, got_t, got_u, got_b, xb, ub, wall, wdn, pre, dall, scl, pb, sb,
    ra, rb, fin, x4, gw, gdn,
    wsem, ts, tr, us, ur, bs_sem, br_sem, zs, zr, rs, rr, gsem,
):
    node = lax.axis_index("node")
    loc = lax.axis_index("local")
    y, x = node // 4, node % 4
    z, c = loc // 2, loc % 2

    def xy_dev(q):
        return (((y + q // 4) % 4) * 4 + (x + q % 4) % 4, loc)

    def z_dev(dz):
        return (node, ((z + dz) % 4) * 2 + c)

    sib = (node, z * 2 + 1 - c)

    loads = []
    for e in range(3):
        loads.append(pltpu.make_async_copy(wg.at[e], wall.at[:, pl.ds(256 * e, 128)], wsem.at[3 * e]))
        loads.append(pltpu.make_async_copy(wu.at[e], wall.at[:, pl.ds(256 * e + 128, 128)], wsem.at[3 * e + 1]))
        loads.append(pltpu.make_async_copy(wd.at[e], wdn.at[pl.ds(128 * e, 128), :], wsem.at[3 * e + 2]))
    for copy in loads:
        copy.start()

    barrier = pltpu.get_barrier_semaphore()
    for q in range(1, 16):
        pl.semaphore_signal(barrier, inc=1, device_id=xy_dev(q), device_id_type=MESH)
    for peer in (z_dev(1), z_dev(3), sib):
        pl.semaphore_signal(barrier, inc=1, device_id=peer, device_id_type=MESH)

    row = iota((256, 128), 0)
    lane = iota((256, 128), 1)
    q = row >> 4
    r = row & 15
    blk = lane >> 4
    g = (((y + (q >> 2)) & 3) << 2) + ((x + (q & 3)) & 3)
    lo = 3 * g
    hit = jnp.zeros((256, 128), F32)
    for k in range(8):
        rk = routes_t[k : k + 1, :]
        hit = jnp.where((rk >= lo) & (rk < lo + 3), 1.0, hit)
    ui = iota((128, 128), 0)
    uj = iota((128, 128), 1)
    before = one_hot(((ui >> 4) == (uj >> 4)) & ((ui & 15) < (uj & 15)))
    place = jnp.dot(hit.astype(BF), before, preferred_element_type=F32).astype(I32)
    want = jnp.where(blk < 3, jnp.where(r < 15, r - 5 * blk, -1), jnp.where(r == 15, blk - 3, -1))
    amat[...] = one_hot((hit > 0.5) & (place == want) & (want >= 0) & (want < 5))

    hot = seq_ids[...] == iota((16, 256), 1)
    seq_w = jnp.sum(jnp.where(hot, jnp.minimum(ratios[...], 1.0), 0.0), axis=1, keepdims=True)
    rw = (combine[...] * seq_w).astype(BF).astype(F32)
    lane16 = iota((16, 128), 1)
    weights = []
    for half in range(2):
        acc = jnp.zeros((16, 128), F32)
        for k in range(8):
            acc = acc + jnp.where(routes[:, k : k + 1] == lane16 - 64 * half, rw[:, k : k + 1], 0.0)
        weights.append(acc.astype(BF))

    def spread(src):
        x3[...] = jnp.zeros((128, PW), BF)
        for j in range(3):
            x3[pl.ds(16 * j, 16), :] = src[:, PW * j : PW * (j + 1)]
        for j in range(5):
            x3[pl.ds(48 + 16 * j, 16), pl.ds(128 * j, 128)] = src[:, 3 * PW : D]

    spread(tok)
    for j in range(5):
        x3[pl.ds(48 + 16 * j, 16), pl.ds(128 * (5 + j // 2), 128)] = weights[j % 2]
    pack_t[...] = jnp.dot(amat[...], x3[...], preferred_element_type=F32).astype(BF)

    pl.semaphore_wait(barrier, 18)

    def xy_copies(src, dst, ssem, rsem):
        return [
            pltpu.make_async_remote_copy(
                src_ref=src.at[pl.ds(16 * k, 16), :],
                dst_ref=dst.at[pl.ds(16 * inverse(k), 16), :],
                send_sem=ssem.at[k],
                recv_sem=rsem.at[inverse(k)],
                device_id=xy_dev(k),
                device_id_type=MESH,
            )
            for k in range(1, 16)
        ]

    sent_t = xy_copies(pack_t, got_t, ts, tr)
    for copy in sent_t:
        copy.start()
    got_t[pl.ds(0, 16), :] = pack_t[pl.ds(0, 16), :]

    spread(ups)
    pack_u[...] = jnp.dot(amat[...], x3[...], preferred_element_type=F32).astype(BF)
    sent_u = xy_copies(pack_u, got_u, us, ur)
    for copy in sent_u:
        copy.start()
    got_u[pl.ds(0, 16), :] = pack_u[pl.ds(0, 16), :]

    brow = iota((4 * ROWS, 256), 0)
    part = jnp.where(brow >= 80, 1, 0) + jnp.where(brow >= 160, 1, 0) + jnp.where(brow >= 240, 1, 0)
    rem = brow - 80 * part
    bq = (rem * 205) >> 10
    bs = rem - 5 * bq
    bmat[...] = one_hot(iota((4 * ROWS, 256), 1) == bq * 16 + jnp.where(part < 3, 5 * part + bs, 15))

    drow = iota((ROWS, 128), 0)
    dlane = iota((ROWS, 128), 1)
    ds_ = drow - 5 * ((drow * 205) >> 10)

    def unpack(got, dst):
        dense = jnp.dot(bmat[...], got[...], preferred_element_type=F32)
        for j in range(3):
            dst[pl.ds(0, ROWS), pl.ds(PW * j, PW)] = dense[ROWS * j : ROWS * (j + 1), :].astype(BF)
        last = dense[3 * ROWS : 4 * ROWS, :]
        tail = jnp.zeros((ROWS, 128), F32)
        for j in range(5):
            tail = jnp.where(ds_ == j, last[:, 128 * j : 128 * (j + 1)], tail)
        dst[pl.ds(0, ROWS), pl.ds(3 * PW, 128)] = tail.astype(BF)
        return last

    def remote(k, src, dst, device, ssem, rsem):
        return pltpu.make_async_remote_copy(
            src_ref=src, dst_ref=dst, send_sem=ssem.at[k], recv_sem=rsem.at[k],
            device_id=device, device_id_type=MESH,
        )

    def gather_copy(k, buf, src, dst, device):
        return remote(k, buf.at[slot(*src), :], buf.at[slot(*dst), :], device, zs, zr)

    tp = gather_copy(0, xb, (0, 0), (3, 0), z_dev(1))
    tm = gather_copy(1, xb, (0, 0), (1, 0), z_dev(3))
    tf = gather_copy(2, xb, (3, 0), (2, 0), z_dev(1))
    t_sib = {dz: gather_copy(3 + dz, xb, (dz, 0), (dz, 1), sib) for dz in range(4)}
    up = gather_copy(7, ub, (0, 0), (3, 0), z_dev(1))
    um = gather_copy(8, ub, (0, 0), (1, 0), z_dev(3))
    uf = gather_copy(9, ub, (1, 0), (2, 0), z_dev(3))
    u_sib = {dz: gather_copy(10 + dz, ub, (dz, 0), (dz, 1), sib) for dz in range(4)}

    for copy in sent_t:
        copy.wait_recv()
    last = unpack(got_t, xb)
    picked = jnp.zeros((ROWS, 128), F32)
    for j in range(5):
        mine = (ds_ == j) & ((dlane >> 6) == j % 2)
        picked = jnp.where(mine, last[:, 128 * (5 + j // 2) : 128 * (6 + j // 2)], picked)
    take = one_hot(((ui & 63) == 3 * node + uj) & (uj < 3))
    xb[pl.ds(0, ROWS), pl.ds(D, 128)] = jnp.dot(picked.astype(BF), take, preferred_element_type=F32).astype(BF)
    tp.start()
    tm.start()
    t_sib[0].start()

    for copy in sent_u:
        copy.wait_recv()
    unpack(got_u, ub)
    up.start()
    um.start()
    u_sib[0].start()

    def compute(r0, m):
        rows = pl.ds(r0, m)
        for e in range(3):
            pre[pl.ds(0, m), pl.ds(256 * e, 256)] = jnp.dot(
                xb[rows, pl.ds(0, D)], wall[:, pl.ds(256 * e, 256)], preferred_element_type=F32
            )
        proj_all = lax.dot_general(ub[rows, :], wdn[...], NT, preferred_element_type=F32)
        score = jnp.zeros((m, 128), F32)
        lanes = iota((m, 128), 1)
        for e in range(3):
            gate = pre[pl.ds(0, m), pl.ds(256 * e, 128)]
            upv = pre[pl.ds(0, m), pl.ds(256 * e + 128, 128)]
            proj = proj_all[:, 128 * e : 128 * (e + 1)]
            scale = xb[rows, pl.ds(D, 128)][:, e : e + 1].astype(F32)
            sig = jax.nn.sigmoid(gate)
            act = gate * sig
            hidden = (act * upv).astype(BF).astype(F32)
            score = jnp.where(lanes == e, jnp.sum(hidden * proj, axis=1, keepdims=True), score)
            dh = scale * proj
            dall[rows, pl.ds(256 * e, 128)] = (dh * upv * sig * (1.0 + gate * (1.0 - sig))).astype(BF)
            dall[rows, pl.ds(256 * e + 128, 128)] = (dh * act).astype(BF)
            scl[rows, pl.ds(128 * e, 128)] = (hidden * scale).astype(BF)
        pb[rows, pl.ds(D, 128)] = score.astype(BF)

        @pl.loop(0, 7)
        def _(i):
            cols = pl.ds(pl.multiple_of(i * 512, 512), 512)
            pb[rows, cols] = lax.dot_general(
                dall[rows, :], wall[cols, :], NT, preferred_element_type=F32
            ).astype(BF)

    p_sib = {
        dz: remote(dz, pb.at[slot(dz, 1), :], sb.at[pl.ds(POS[dz] * ROWS, ROWS), :], sib, rs, rr)
        for dz in range(4)
    }

    def pair_sum(dz):
        p_sib[dz].wait_recv()
        pb[slot(dz, 0), :] = (
            pb[slot(dz, 0), :].astype(F32) + sb[pl.ds(POS[dz] * ROWS, ROWS), :].astype(F32)
        ).astype(BF)

    for copy in loads:
        copy.wait()
    t_sib[0].wait_recv()
    u_sib[0].wait_recv()
    compute(0, 160)
    p_sib[0].start()

    tp.wait_recv()
    tf.start()
    t_sib[3].start()
    tm.wait_recv()
    t_sib[1].start()
    um.wait_recv()
    uf.start()
    u_sib[1].start()
    up.wait_recv()
    u_sib[3].start()
    for dz in (1, 3):
        t_sib[dz].wait_recv()
        u_sib[dz].wait_recv()
    compute(160, 320)
    p_sib[1].start()
    p_sib[3].start()

    tf.wait_recv()
    t_sib[2].start()
    uf.wait_recv()
    u_sib[2].start()
    t_sib[2].wait_recv()
    u_sib[2].wait_recv()
    compute(480, 160)
    p_sib[2].start()

    first = pl.ds(0, CA)
    second = pl.ds(CA, DT - CA)
    q2a = remote(4, pb.at[slot(2, 0), first], ra, z_dev(1), rs, rr)
    q2b = remote(5, pb.at[slot(2, 0), second], rb, z_dev(3), rs, rr)
    r1a = remote(6, pb.at[slot(1, 0), first], fin.at[0, :, first], z_dev(1), rs, rr)
    r1b = remote(7, pb.at[slot(1, 0), second], fin.at[0, :, second], z_dev(1), rs, rr)
    r3a = remote(8, pb.at[slot(3, 0), first], fin.at[1, :, first], z_dev(3), rs, rr)
    r3b = remote(9, pb.at[slot(3, 0), second], fin.at[1, :, second], z_dev(3), rs, rr)

    pair_sum(2)
    q2a.start()
    q2b.start()
    pair_sum(1)
    r1b.start()
    pair_sum(3)
    r3a.start()

    def weight_grads(lo_, hi_):
        @pl.loop(lo_, hi_)
        def _(i):
            cols = pl.ds(pl.multiple_of(i * 512, 512), 512)
            gw[cols, :] = lax.dot_general(xb[:, cols], dall[...], TN, preferred_element_type=F32).astype(BF)

    def down_grads(lo_, hi_):
        @pl.loop(lo_, hi_)
        def _(i):
            cols = pl.ds(pl.multiple_of(i * 512, 512), 512)
            gdn[:, cols] = lax.dot_general(scl[...], ub[:, cols], TN, preferred_element_type=F32).astype(BF)

    weight_grads(0, 7)
    q2a.wait_recv()
    pb[slot(1, 0), first] = (pb[slot(1, 0), first].astype(F32) + ra[...].astype(F32)).astype(BF)
    r1a.start()
    q2b.wait_recv()
    pb[slot(3, 0), second] = (pb[slot(3, 0), second].astype(F32) + rb[...].astype(F32)).astype(BF)
    r3b.start()

    outs = []
    for e in range(3):
        outs.append(pltpu.make_async_copy(gw.at[:, pl.ds(256 * e, 128)], gg.at[e], gsem.at[e]))
        outs.append(pltpu.make_async_copy(gw.at[:, pl.ds(256 * e + 128, 128)], gu.at[e], gsem.at[3 + e]))
    for copy in outs:
        copy.start()
    down_grads(0, 7)
    downs = [
        pltpu.make_async_copy(gdn.at[pl.ds(128 * e, 128), :], gd.at[e], gsem.at[6 + e]) for e in range(3)
    ]
    for copy in downs:
        copy.start()

    pair_sum(0)
    for copy in (r1b, r3a, r1a, r3b):
        copy.wait_recv()
    total = pb[slot(0, 0), :].astype(F32) + fin[0].astype(F32) + fin[1].astype(F32)
    x4[...] = jnp.zeros((384, PW), BF)
    for j in range(3):
        x4[pl.ds(ROWS * j, ROWS), :] = total[:, PW * j : PW * (j + 1)].astype(BF)
    tail = total[:, 3 * PW : D]
    for j in range(5):
        x4[pl.ds(3 * ROWS, ROWS), pl.ds(128 * j, 128)] = jnp.where(ds_ == j, tail, 0.0).astype(BF)
    repeat = one_hot((ui == (uj & 7)) & (ui < 3))
    score = jnp.dot(total[:, D:DT].astype(BF), repeat, preferred_element_type=F32)
    x4[pl.ds(3 * ROWS, ROWS), pl.ds(640, 128)] = jnp.where((dlane >> 3) == ds_, score, 0.0).astype(BF)
    crow = iota((256, 384), 0)
    clane = iota((256, 384), 1)
    cpart = jnp.where(clane >= 80, 1, 0) + jnp.where(clane >= 160, 1, 0) + jnp.where(clane >= 240, 1, 0)
    crem = clane - 80 * cpart
    cq = (crem * 205) >> 10
    cs = crem - 5 * cq
    cmat = one_hot((crow == cq * 16 + jnp.where(cpart < 3, 5 * cpart + cs, 15)) & (clane < 320))
    pack_b[...] = jnp.dot(cmat, x4[...], preferred_element_type=F32).astype(BF)
    sent_b = xy_copies(pack_b, got_b, bs_sem, br_sem)
    for copy in sent_b:
        copy.start()
    got_b[pl.ds(0, 16), :] = pack_b[pl.ds(0, 16), :]
    for copy in sent_b:
        copy.wait_recv()

    summed = lax.dot_general(amat[...], got_b[...], TN, preferred_element_type=F32)
    for j in range(3):
        gt[:, pl.ds(PW * j, PW)] = summed[16 * j : 16 * (j + 1), :].astype(BF)
    tail = jnp.zeros((16, 128), F32)
    for j in range(5):
        tail = tail + summed[48 + 16 * j : 64 + 16 * j, 128 * j : 128 * (j + 1)]
    gt[:, pl.ds(3 * PW, 128)] = tail.astype(BF)

    third = uj - 3 * ((uj * 171) >> 9)
    token_score = jnp.zeros((16, 128), F32)
    for j in range(5):
        pick = one_hot(ui == 8 * j + third)
        wide = jnp.dot(got_b[:, pl.ds(640, 128)], pick, preferred_element_type=F32)
        wide = jnp.where((lane >= lo) & (lane < lo + 3), wide, 0.0).astype(BF)
        share = lax.dot_general(amat[...], wide, TN, preferred_element_type=F32)
        token_score = token_score + share[48 + 16 * j : 64 + 16 * j, :]
    result = jnp.zeros((16, 128), F32)
    for k in range(8):
        value = jnp.sum(jnp.where(routes[:, k : k + 1] == lane16, token_score, 0.0), axis=1, keepdims=True)
        result = jnp.where(lane16 == k, value * seq_w, result)
    gc[...] = result[:, :8]

    for copy in sent_t + sent_u + sent_b:
        copy.wait_send()
    for copy in (tp, tm, tf, up, um, uf, q2a, q2b, r1a, r1b, r3a, r3b):
        copy.wait_send()
    for dz in range(4):
        t_sib[dz].wait_send()
        u_sib[dz].wait_send()
        p_sib[dz].wait_send()
    for copy in outs + downs:
        copy.wait()


def local(tokens, upstream, routes, combine, seq_ids, ratios, w_gate, w_up, w_down):
    vmem = pl.BlockSpec(memory_space=pltpu.VMEM)
    hbm = pl.BlockSpec(memory_space=pl.ANY)
    shape = jax.ShapeDtypeStruct
    dma = pltpu.SemaphoreType.DMA
    return pl.pallas_call(
        kernel,
        out_shape=(
            shape((16, D), BF),
            shape((16, 8), F32),
            shape((3, D, 128), BF),
            shape((3, D, 128), BF),
            shape((3, 128, D), BF),
        ),
        in_specs=[vmem] * 7 + [hbm] * 3,
        out_specs=(vmem, vmem, hbm, hbm, hbm),
        scratch_shapes=[
            pltpu.VMEM((256, 128), BF),
            pltpu.VMEM((320, 256), BF),
            pltpu.VMEM((128, PW), BF),
            pltpu.VMEM((256, PW), BF),
            pltpu.VMEM((256, PW), BF),
            pltpu.VMEM((256, PW), BF),
            pltpu.VMEM((256, PW), BF),
            pltpu.VMEM((256, PW), BF),
            pltpu.VMEM((256, PW), BF),
            pltpu.VMEM((640, DT), BF),
            pltpu.VMEM((640, D), BF),
            pltpu.VMEM((D, 768), BF),
            pltpu.VMEM((384, D), BF),
            pltpu.VMEM((320, 768), F32),
            pltpu.VMEM((640, 768), BF),
            pltpu.VMEM((640, 384), BF),
            pltpu.VMEM((640, DT), BF),
            pltpu.VMEM((320, DT), BF),
            pltpu.VMEM((ROWS, CA), BF),
            pltpu.VMEM((ROWS, DT - CA), BF),
            pltpu.VMEM((2, ROWS, DT), BF),
            pltpu.VMEM((384, PW), BF),
            pltpu.VMEM((D, 768), BF),
            pltpu.VMEM((384, D), BF),
            dma((9,)),
            dma((16,)), dma((16,)), dma((16,)), dma((16,)), dma((16,)), dma((16,)),
            dma((14,)), dma((14,)), dma((10,)), dma((10,)), dma((9,)),
        ],
        compiler_params=pltpu.CompilerParams(
            collective_id=0, has_side_effects=True, vmem_limit_bytes=58 << 20
        ),
        name="moe_grad",
    )(
        tokens, upstream, routes, jnp.tile(routes.T, (1, 8)), combine,
        seq_ids[:, None], ratios[None, :], w_gate, w_up, w_down,
    )


def solution(mesh):
    rows = P(("node", "local"), None)
    return jax.shard_map(
        local,
        mesh=mesh,
        in_specs=(
            rows, rows, rows, rows, P(("node", "local")), P(),
            P("node", None, "local"), P("node", None, "local"), P("node", "local", None),
        ),
        out_specs=(rows, rows, P("node", None, "local"), P("node", None, "local"), P("node", "local", None)),
        check_vma=False,
    )
```

time: 438 us -> 118 us (0.27)
  waiting for transfers between devices: 237 us -> 0 us
  Pallas kernels: 0 us -> 101 us
  matrix products: 94.8 us -> 0 us
  starting transfers between devices: 42.1 us -> 0 us
  local copies, waits for them, and re-layouts: 42 us -> 16.3 us
  other arithmetic: 16.7 us -> 0 us
    all_to_all x5 -> x0, waiting for transfers between devices: 237 us -> none  [the longest x1 89.1 us: local(): lax.all_to_all(spread(send_tokens), ('node', 'local'), split_axis=0, conc...]
    pallas_call x0 -> x1, Pallas kernels: none -> 101 us  [local(): pl.pallas_call(kernel, out_shape=(shape((16, D), BF), shape((16, 8), F32)...]
    dot_general x29 -> x0, matrix products: 94.8 us -> none  [the longest x3 29 us: local(): lax.dot_general(d_up, w_up[expert], contract_last, preferred_element_type...]
    all_to_all x5 -> x0, starting transfers between devices: 42.1 us -> none  [the longest x1 11.9 us: local(): lax.all_to_all(spread(send_tokens), ('node', 'local'), split_axis=0, conc...]
    reshape x4 -> x0, local copies, waits for them, and re-layouts: 24.2 us -> none  [the longest x1 8.25 us: local(): in_rows = arrived[0].reshape(-1, features)]
    unnamed x77 -> x10, local copies, waits for them, and re-layouts: 3.4 us -> 12.2 us
    broadcast_in_dim x5 -> x1, local copies, waits for them, and re-layouts: 7.75 us -> 1.33 us  [local(): seq_ids[:, None]]
    reduce_sum x4 -> x0, other arithmetic: 6.41 us -> none  [the longest x1 4.55 us: local(): jnp.sum(returned[0].astype(jnp.float32).reshape(node_count, local_count,...]
  transfers between devices with their start and end apart: 5 -> 0, of which waited for: 5 -> 0; matrix products, arithmetic and copies ran while one was open for 12% -> 0% of each run, Pallas kernels for 0% -> 0%
where the time goes in v1:
time: 118 us
  Pallas kernels  101 us (86%)
  local copies, waits for them, and re-layouts  16.3 us (14%)
    pallas_call x1, Pallas kernels, local(): pl.pallas_call(kernel, out_shape=(shape((16, D), BF), shape((16, 8), F32)...  101 us
    unnamed x10, local copies, waits for them, and re-layouts  12.2 us

profile of v1, /device:TPU:1, one launch (start us, length us, event | category | flops | bytes accessed | tf_op | source)
XLA Modules:
  0.0 117.6 jit_solution(14630443367409129103)
XLA Ops:
  0.6 1.4 %copy.15.combine = f32[16,8]{1,0:T(8,128)} copy(f32[16,8]{0,1:T(8,128)} %param.12) | data formatting | bytes 1024 | tf_op args[3]
  2.0 1.3 %copy.16.seq_ids = s32[16,1]{1,0:T(8,128)} copy(s32[16,1]{0,1:T(1,128)} %bitcast.5) | data formatting | bytes 128 | tf_op jit(solution)/shard_map/broadcast_in_dim | solution.py:439
  3.3 1.4 %copy.14.routes = s32[16,8]{1,0:T(8,128)} copy(s32[16,8]{0,1:T(8,128)} %param.11) | data formatting | bytes 1024 | tf_op args[2]
  4.7 0.7 tile.4
  5.4 0.7 tile.10.routes_t
  6.0 100.7 %moe_grad.1 = (bf16[16,3584]{1,0:T(8,128)(2,1)}, f32[16,8]{1,0:T(8,128)}, bf16[3,3584,128]{2,1,0:T(8,128)(2,1)}, bf16[3,3584,128]{2,1,0:T(8,128)(2,1)}, bf16[3,128,3584]{2,1,0:T(8,128)(2,1)}) custom-call(bf16[16,3584]{1,0:T(8,128)(2,1)} %tok.1, bf16[16,3584]{1,0:T(8,128)(2,1)} %ups.1, s32[16,8]{1,0:T(8,128)} %copy.14.routes, s32[8,128]{1,0:T(8,128)} %tile.10.routes_t, ...), custom_call_target="tpu_custom_call" | custom-call | tf_op jit(solution)/shard_map/moe_grad/pallas_call | solution.py:393
  106.8 1.4 %copy.17 = f32[16,8]{0,1:T(8,128)} copy(f32[16,8]{1,0:T(8,128)} %get-tuple-element.6) | data formatting | bytes 1024 | tf_op jit(solution)/shard_map/moe_grad/pallas_call | solution.py:393
  108.1 1.6 %copy.22 = bf16[16,3584]{1,0:T(8,128)(2,1)} copy(bf16[16,3584]{1,0:T(8,128)(2,1)} %get-tuple-element.15) | data formatting | bytes 229376
  109.7 0.0 copy-start.1
  109.7 3.6 %copy.23 = bf16[3,3584,128]{2,1,0:T(8,128)(2,1)} copy(bf16[3,3584,128]{2,1,0:T(8,128)(2,1)} %get-tuple-element.17) | data formatting | bytes 5505024
  113.3 0.0 copy-done.1
  113.3 0.0 copy-start
  113.3 1.5 %copy.24 = bf16[3,3584,128]{2,1,0:T(8,128)(2,1)} copy(bf16[3,3584,128]{2,1,0:T(8,128)(2,1)S(1)} %copy-done.1) | data formatting | bytes 5505024
  114.9 1.2 %copy-done = bf16[3,128,3584]{2,1,0:T(8,128)(2,1)S(1)} copy-done((bf16[3,128,3584]{2,1,0:T(8,128)(2,1)S(1)}, bf16[3,128,3584]{2,1,0:T(8,128)(2,1)}, u32[]{:S(2)}) %copy-start) | copy-done | bytes 2752536
  116.1 1.5 %copy.25 = bf16[3,128,3584]{2,1,0:T(8,128)(2,1)} copy(bf16[3,128,3584]{2,1,0:T(8,128)(2,1)S(1)} %copy-done) | data formatting | bytes 5505024
Async XLA Ops:
  109.7 3.6 %copy-start.1 = (bf16[3,3584,128]{2,1,0:T(8,128)(2,1)S(1)}, bf16[3,3584,128]{2,1,0:T(8,128)(2,1)}, u32[]{:S(2)}) copy-start(bf16[3,3584,128]{2,1,0:T(8,128)(2,1)} %get-tuple-element.18) | copy-start | bytes 8257540
  113.3 2.8 %copy-start = (bf16[3,128,3584]{2,1,0:T(8,128)(2,1)S(1)}, bf16[3,128,3584]{2,1,0:T(8,128)(2,1)}, u32[]{:S(2)}) copy-start(bf16[3,128,3584]{2,1,0:T(8,128)(2,1)} %get-tuple-element.19) | copy-start | bytes 8257540

commit v2 on v1

--- a/solution.py
+++ b/solution.py
@@ -36,12 +36,18 @@
     return jnp.where(mask, 1.0, 0.0).astype(BF)
 
 
+def seq_weight(seq_ids, ratios):
+    hot = jnp.where(iota((256, 16), 0) == seq_ids[...], 1.0, 0.0)
+    clipped = jnp.broadcast_to(jnp.minimum(ratios[...], 1.0), (8, 256))
+    return jnp.dot(clipped, hot, precision=lax.Precision.HIGHEST, preferred_element_type=F32)
+
+
 def kernel(
-    tok, ups, routes, routes_t, combine, seq_ids, ratios, wg, wu, wd,
-    gt, gc, gg, gu, gd,
-    amat, bmat, x3, pack_t, pack_u, pack_b, got_t, got_u, got_b, xb, ub, wall, wdn, pre, dall, scl, pb, sb,
-    ra, rb, fin, x4, gw, gdn,
-    wsem, ts, tr, us, ur, bs_sem, br_sem, zs, zr, rs, rr, gsem,
+    tok, ups, routes_t, combine_t, seq_ids, ratios, wg, wu, wd,
+    amat, got_b, gg, gu, gd,
+    bmat, x3, pack_t, pack_u, pack_b, got_t, got_u, xb, ub, wall, wdn, pre, dall, scl, pb, sb,
+    ra, rb, fin, x4,
+    wsem, ts, tr, us, ur, bs_sem, br_sem, zs, zr, rs, rr,
 ):
     node = lax.axis_index("node")
     loc = lax.axis_index("local")
@@ -69,6 +75,14 @@
         pl.semaphore_signal(barrier, inc=1, device_id=xy_dev(q), device_id_type=MESH)
     for peer in (z_dev(1), z_dev(3), sib):
         pl.semaphore_signal(barrier, inc=1, device_id=peer, device_id_type=MESH)
+
+    seq_w = seq_weight(seq_ids, ratios)
+    rw = (combine_t[...] * seq_w).astype(BF).astype(F32)
+    tiled = jnp.dot(
+        routes_t[...].astype(F32).astype(BF),
+        one_hot((iota((16, 128), 1) & 15) == iota((16, 128), 0)),
+        preferred_element_type=F32,
+    ).astype(I32)
 
     row = iota((256, 128), 0)
     lane = iota((256, 128), 1)
@@ -79,7 +93,7 @@
     lo = 3 * g
     hit = jnp.zeros((256, 128), F32)
     for k in range(8):
-        rk = routes_t[k : k + 1, :]
+        rk = tiled[k : k + 1, :]
         hit = jnp.where((rk >= lo) & (rk < lo + 3), 1.0, hit)
     ui = iota((128, 128), 0)
     uj = iota((128, 128), 1)
@@ -88,16 +102,16 @@
     want = jnp.where(blk < 3, jnp.where(r < 15, r - 5 * blk, -1), jnp.where(r == 15, blk - 3, -1))
     amat[...] = one_hot((hit > 0.5) & (place == want) & (want >= 0) & (want < 5))
 
-    hot = seq_ids[...] == iota((16, 256), 1)
-    seq_w = jnp.sum(jnp.where(hot, jnp.minimum(ratios[...], 1.0), 0.0), axis=1, keepdims=True)
-    rw = (combine[...] * seq_w).astype(BF).astype(F32)
-    lane16 = iota((16, 128), 1)
+    expert = iota((128, 16), 0)
+    same = one_hot(ui == uj)
     weights = []
     for half in range(2):
-        acc = jnp.zeros((16, 128), F32)
+        acc = jnp.zeros((128, 16), F32)
         for k in range(8):
-            acc = acc + jnp.where(routes[:, k : k + 1] == lane16 - 64 * half, rw[:, k : k + 1], 0.0)
-        weights.append(acc.astype(BF))
+            acc = acc + jnp.where(routes_t[k : k + 1, :] == expert - 64 * half, rw[k : k + 1, :], 0.0)
+        weights.append(
+            lax.dot_general(acc.astype(BF), same, TN, preferred_element_type=F32).astype(BF)
+        )
 
     def spread(src):
         x3[...] = jnp.zeros((128, PW), BF)
@@ -294,13 +308,18 @@
         @pl.loop(lo_, hi_)
         def _(i):
             cols = pl.ds(pl.multiple_of(i * 512, 512), 512)
-            gw[cols, :] = lax.dot_general(xb[:, cols], dall[...], TN, preferred_element_type=F32).astype(BF)
+            grads = lax.dot_general(xb[:, cols], dall[...], TN, preferred_element_type=F32).astype(BF)
+            for e in range(3):
+                gg[e, cols, :] = grads[:, 256 * e : 256 * e + 128]
+                gu[e, cols, :] = grads[:, 256 * e + 128 : 256 * (e + 1)]
 
     def down_grads(lo_, hi_):
         @pl.loop(lo_, hi_)
         def _(i):
             cols = pl.ds(pl.multiple_of(i * 512, 512), 512)
-            gdn[:, cols] = lax.dot_general(scl[...], ub[:, cols], TN, preferred_element_type=F32).astype(BF)
+            grads = lax.dot_general(scl[...], ub[:, cols], TN, preferred_element_type=F32).astype(BF)
+            for e in range(3):
+                gd[e, :, cols] = grads[128 * e : 128 * (e + 1), :]
 
     weight_grads(0, 7)
     q2a.wait_recv()
@@ -310,18 +329,7 @@
     pb[slot(3, 0), second] = (pb[slot(3, 0), second].astype(F32) + rb[...].astype(F32)).astype(BF)
     r3b.start()
 
-    outs = []
-    for e in range(3):
-        outs.append(pltpu.make_async_copy(gw.at[:, pl.ds(256 * e, 128)], gg.at[e], gsem.at[e]))
-        outs.append(pltpu.make_async_copy(gw.at[:, pl.ds(256 * e + 128, 128)], gu.at[e], gsem.at[3 + e]))
-    for copy in outs:
-        copy.start()
     down_grads(0, 7)
-    downs = [
-        pltpu.make_async_copy(gdn.at[pl.ds(128 * e, 128), :], gd.at[e], gsem.at[6 + e]) for e in range(3)
-    ]
-    for copy in downs:
-        copy.start()
 
     pair_sum(0)
     for copy in (r1b, r3a, r1a, r3b):
@@ -351,6 +359,32 @@
     for copy in sent_b:
         copy.wait_recv()
 
+    for copy in sent_t + sent_u + sent_b:
+        copy.wait_send()
+    for copy in (tp, tm, tf, up, um, uf, q2a, q2b, r1a, r1b, r3a, r3b):
+        copy.wait_send()
+    for dz in range(4):
+        t_sib[dz].wait_send()
+        u_sib[dz].wait_send()
+        p_sib[dz].wait_send()
+
+
+def finish(amat, got_b, routes_t, seq_ids, ratios, gg_in, gu_in, gd_in, gt, gc, gg, gu, gd, sems):
+    copies = []
+    for k, (src, dst) in enumerate(((gg_in, gg), (gu_in, gu), (gd_in, gd))):
+        for e in range(3):
+            copies.append(pltpu.make_async_copy(src.at[e], dst.at[e], sems.at[3 * k + e]))
+    for copy in copies:
+        copy.start()
+    node = lax.axis_index("node")
+    y, x = node // 4, node % 4
+    row = iota((256, 128), 0)
+    lane = iota((256, 128), 1)
+    q = row >> 4
+    lo = 3 * ((((y + (q >> 2)) & 3) << 2) + ((x + (q & 3)) & 3))
+    ui = iota((128, 128), 0)
+    uj = iota((128, 128), 1)
+    seq_w = seq_weight(seq_ids, ratios)
     summed = lax.dot_general(amat[...], got_b[...], TN, preferred_element_type=F32)
     for j in range(3):
         gt[:, pl.ds(PW * j, PW)] = summed[16 * j : 16 * (j + 1), :].astype(BF)
@@ -367,21 +401,13 @@
         wide = jnp.where((lane >= lo) & (lane < lo + 3), wide, 0.0).astype(BF)
         share = lax.dot_general(amat[...], wide, TN, preferred_element_type=F32)
         token_score = token_score + share[48 + 16 * j : 64 + 16 * j, :]
-    result = jnp.zeros((16, 128), F32)
+    eye = one_hot(iota((16, 16), 0) == iota((16, 16), 1))
+    scores = lax.dot_general(token_score.astype(BF), eye, TN, preferred_element_type=F32)
+    expert = iota((128, 16), 0)
     for k in range(8):
-        value = jnp.sum(jnp.where(routes[:, k : k + 1] == lane16, token_score, 0.0), axis=1, keepdims=True)
-        result = jnp.where(lane16 == k, value * seq_w, result)
-    gc[...] = result[:, :8]
-
-    for copy in sent_t + sent_u + sent_b:
-        copy.wait_send()
-    for copy in (tp, tm, tf, up, um, uf, q2a, q2b, r1a, r1b, r3a, r3b):
-        copy.wait_send()
-    for dz in range(4):
-        t_sib[dz].wait_send()
-        u_sib[dz].wait_send()
-        p_sib[dz].wait_send()
-    for copy in outs + downs:
+        value = jnp.sum(jnp.where(routes_t[k : k + 1, :] == expert, scores, 0.0), axis=0, keepdims=True)
+        gc[pl.ds(k, 1), :] = value * seq_w[k : k + 1, :]
+    for copy in copies:
         copy.wait()
 
 
@@ -390,22 +416,21 @@
     hbm = pl.BlockSpec(memory_space=pl.ANY)
     shape = jax.ShapeDtypeStruct
     dma = pltpu.SemaphoreType.DMA
-    return pl.pallas_call(
+    routes_t, combine_t, seq_ids, ratios = routes.T, combine.T, seq_ids[None, :], ratios[None, :]
+    amat, got_b, *grads = pl.pallas_call(
         kernel,
         out_shape=(
-            shape((16, D), BF),
-            shape((16, 8), F32),
-            shape((3, D, 128), BF),
-            shape((3, D, 128), BF),
-            shape((3, 128, D), BF),
+            pltpu.VMEM((256, 128), BF),
+            pltpu.VMEM((256, PW), BF),
+            pltpu.VMEM((3, D, 128), BF),
+            pltpu.VMEM((3, D, 128), BF),
+            pltpu.VMEM((3, 128, D), BF),
         ),
-        in_specs=[vmem] * 7 + [hbm] * 3,
-        out_specs=(vmem, vmem, hbm, hbm, hbm),
+        in_specs=[vmem] * 6 + [hbm] * 3,
+        out_specs=(vmem,) * 5,
         scratch_shapes=[
-            pltpu.VMEM((256, 128), BF),
             pltpu.VMEM((320, 256), BF),
             pltpu.VMEM((128, PW), BF),
-            pltpu.VMEM((256, PW), BF),
             pltpu.VMEM((256, PW), BF),
             pltpu.VMEM((256, PW), BF),
             pltpu.VMEM((256, PW), BF),
@@ -424,20 +449,31 @@
             pltpu.VMEM((ROWS, DT - CA), BF),
             pltpu.VMEM((2, ROWS, DT), BF),
             pltpu.VMEM((384, PW), BF),
-            pltpu.VMEM((D, 768), BF),
-            pltpu.VMEM((384, D), BF),
             dma((9,)),
             dma((16,)), dma((16,)), dma((16,)), dma((16,)), dma((16,)), dma((16,)),
-            dma((14,)), dma((14,)), dma((10,)), dma((10,)), dma((9,)),
+            dma((14,)), dma((14,)), dma((10,)), dma((10,)),
         ],
         compiler_params=pltpu.CompilerParams(
-            collective_id=0, has_side_effects=True, vmem_limit_bytes=58 << 20
+            collective_id=0, has_side_effects=True, vmem_limit_bytes=46 << 20
         ),
         name="moe_grad",
-    )(
-        tokens, upstream, routes, jnp.tile(routes.T, (1, 8)), combine,
-        seq_ids[:, None], ratios[None, :], w_gate, w_up, w_down,
-    )
+    )(tokens, upstream, routes_t, combine_t, seq_ids, ratios, w_gate, w_up, w_down)
+    gt, gc, gg, gu, gd = pl.pallas_call(
+        finish,
+        out_shape=(
+            shape((16, D), BF),
+            shape((8, 16), F32),
+            shape((3, D, 128), BF),
+            shape((3, D, 128), BF),
+            shape((3, 128, D), BF),
+        ),
+        in_specs=[vmem] * 8,
+        out_specs=(vmem, vmem, hbm, hbm, hbm),
+        scratch_shapes=[dma((9,))],
+        compiler_params=pltpu.CompilerParams(vmem_limit_bytes=16 << 20),
+        name="moe_finish",
+    )(amat, got_b, routes_t, seq_ids, ratios, *grads)
+    return gt, gc.T, gg, gu, gd
 
 
 def solution(mesh):

time: 118 us -> 104 us (0.88)
  local copies, waits for them, and re-layouts: 16.3 us -> 0.01 us
  Pallas kernels: 101 us -> 104 us
    unnamed x10 -> x6, local copies, waits for them, and re-layouts: 12.2 us -> 0.01 us
    pallas_call x1 -> x2, Pallas kernels: 101 us -> 104 us  [the longest x1 99.3 us: local(): pl.pallas_call(kernel, out_shape=(pltpu.VMEM((256, 128), BF), pltpu.VMEM(...]
    another operation x2 -> x0, local copies, waits for them, and re-layouts: 1.36 us -> none  [local(): jnp.tile(routes.T, (1, 8))]
    pallas_call x1 -> x0, local copies, waits for them, and re-layouts: 1.36 us -> none  [local(): pl.pallas_call(kernel, out_shape=(shape((16, D), BF), shape((16, 8), F32)...]
    broadcast_in_dim x1 -> x0, local copies, waits for them, and re-layouts: 1.33 us -> none  [local(): seq_ids[:, None]]
where the time goes in v2:
time: 104 us
  Pallas kernels  104 us (100%)
    pallas_call x1, Pallas kernels, local(): pl.pallas_call(kernel, out_shape=(pltpu.VMEM((256, 128), BF), pltpu.VMEM(...  99.3 us
    pallas_call x1, Pallas kernels, local(): pl.pallas_call(finish, out_shape=(shape((16, D), BF), shape((8, 16), F32)...  4.23 us

profile of v2, /device:TPU:1, one launch (start us, length us, event | category | flops | bytes accessed | tf_op | source)
XLA Modules:
  0.0 104.3 jit_solution(17492990478939080471)
XLA Ops:
  0.6 0.0 copy-start
  0.6 0.0 copy-start.1
  0.7 0.0 copy-start.2
  0.7 99.3 %moe_grad.1 = (bf16[256,128]{1,0:T(8,128)(2,1)S(1)}, bf16[256,1152]{1,0:T(8,128)(2,1)S(1)}, bf16[3,3584,128]{2,1,0:T(8,128)(2,1)S(1)}, bf16[3,3584,128]{2,1,0:T(8,128)(2,1)S(1)}, bf16[3,128,3584]{2,1,0:T(8,128)(2,1)S(1)}) custom-call(bf16[16,3584]{1,0:T(8,128)(2,1)} %tok.1, bf16[16,3584]{1,0:T(8,128)(2,1)} %ups.1, s32[8,16]{1,0:T(8,128)} %bitcast.5, ...), custom_call_target="tpu_custom_call" | custom-call | tf_op jit(solution)/shard_map/moe_grad/pallas_call | solution.py:420
  100.0 0.0 copy-done
  100.0 0.0 copy-done.1
  100.0 0.0 copy-done.2
  100.0 4.2 %moe_finish.1 = (bf16[16,3584]{1,0:T(8,128)(2,1)}, f32[8,16]{1,0:T(8,128)}, bf16[3,3584,128]{2,1,0:T(8,128)(2,1)}, bf16[3,3584,128]{2,1,0:T(8,128)(2,1)}, bf16[3,128,3584]{2,1,0:T(8,128)(2,1)}) custom-call(bf16[256,128]{1,0:T(8,128)(2,1)S(1)} %get-tuple-element.15.amat, bf16[256,1152]{1,0:T(8,128)(2,1)S(1)} %get-tuple-element.16.got_b, s32[8,16]{1,0:T(8,128)S(1)} %bitcast.6, ...), custom_call_target="tpu_custom_call" | custom-call | tf_op jit(solution)/shard_map/moe_finish/pallas_call | solution.py:461
Async XLA Ops:
  0.6 99.4 %copy-start = (s32[16,8]{0,1:T(8,128)S(1)}, s32[16,8]{0,1:T(8,128)}, u32[]{:S(2)}) copy-start(s32[16,8]{0,1:T(8,128)} %param.11) | copy-start | bytes 1540
  0.6 99.4 %copy-start.1 = (f32[256]{0:T(256)S(1)}, f32[256]{0:T(256)}, u32[]{:S(2)}) copy-start(f32[256]{0:T(256)} %param.14) | copy-start | bytes 3076
  0.7 99.4 %copy-start.2 = (s32[16]{0:T(128)S(1)}, s32[16]{0:T(128)}, u32[]{:S(2)}) copy-start(s32[16]{0:T(128)} %param.13) | copy-start | bytes 196

commit v3 on v2

v3 whole, which is shorter than its diff:
```python
import jax
import jax.numpy as jnp
from jax import lax
from jax.experimental import pallas as pl
from jax.experimental.pallas import tpu as pltpu
from jax.sharding import PartitionSpec as P

MESH = pl.DeviceIdType.MESH
BF = jnp.bfloat16
F32 = jnp.float32
I32 = jnp.int32

D = 3584
DT = D + 128
PW = 1152
ROWS = 80
POS = {0: 0, 1: 1, 3: 2, 2: 3}
NEAR = (1, 3, 4, 12, 2, 5, 7, 8, 13, 15, 6, 9, 11, 14, 10)
NT = (((1,), (1,)), ((), ()))
TN = (((0,), (0,)), ((), ()))


def slot(dz, dc):
    return pl.ds((POS[dz] * 2 + dc) * ROWS, ROWS)


def inverse(q):
    return ((-(q // 4)) % 4) * 4 + (-(q % 4)) % 4


def iota(shape, dim):
    return lax.broadcasted_iota(I32, shape, dim)


def one_hot(mask):
    return jnp.where(mask, 1.0, 0.0).astype(BF)


def seq_weight(seq_ids, ratios):
    hot = jnp.where(iota((256, 16), 0) == seq_ids[...], 1.0, 0.0)
    clipped = jnp.broadcast_to(jnp.minimum(ratios[...], 1.0), (8, 256))
    return jnp.dot(clipped, hot, precision=lax.Precision.HIGHEST, preferred_element_type=F32)


def route_matrix(tiled, y, x):
    row = iota((256, 128), 0)
    lane = iota((256, 128), 1)
    r = row & 15
    blk = lane >> 4
    lo = first_expert(row, y, x)
    hit = jnp.zeros((256, 128), F32)
    for k in range(8):
        rk = tiled[k : k + 1, :]
        hit = jnp.where((rk >= lo) & (rk < lo + 3), 1.0, hit)
    ui = iota((128, 128), 0)
    uj = iota((128, 128), 1)
    before = one_hot(((ui >> 4) == (uj >> 4)) & ((ui & 15) < (uj & 15)))
    place = jnp.dot(hit.astype(BF), before, preferred_element_type=F32).astype(I32)
    want = jnp.where(blk < 3, jnp.where(r < 15, r - 5 * blk, -1), jnp.where(r == 15, blk - 3, -1))
    return one_hot((hit > 0.5) & (place == want) & (want >= 0) & (want < 5))


def first_expert(row, y, x):
    q = row >> 4
    return 3 * ((((y + (q >> 2)) & 3) << 2) + ((x + (q & 3)) & 3))


def token_sums(amat, got, y, x):
    row = iota((256, 128), 0)
    lane = iota((256, 128), 1)
    lo = first_expert(row, y, x)
    summed = lax.dot_general(amat[...], got[...], TN, preferred_element_type=F32)
    parts = [summed[16 * j : 16 * (j + 1), :] for j in range(3)]
    tail = jnp.zeros((16, 128), F32)
    for j in range(5):
        tail = tail + summed[48 + 16 * j : 64 + 16 * j, 128 * j : 128 * (j + 1)]
    ui = iota((128, 128), 0)
    uj = iota((128, 128), 1)
    third = uj - 3 * ((uj * 171) >> 9)
    score = jnp.zeros((16, 128), F32)
    for j in range(5):
        pick = one_hot(ui == 8 * j + third)
        wide = jnp.dot(got[:, pl.ds(640, 128)], pick, preferred_element_type=F32)
        wide = jnp.where((lane >= lo) & (lane < lo + 3), wide, 0.0).astype(BF)
        share = lax.dot_general(amat[...], wide, TN, preferred_element_type=F32)
        score = score + share[48 + 16 * j : 64 + 16 * j, :]
    return parts, tail, score


def kernel(
    tok, ups, routes_t, combine_t, seq_ids, ratios, wg, wu, wd,
    amat, got_b, far, gg, gu, gd,
    amat2, bmat, cmat, x3, info, tok2, ups2, info2, far_out,
    pack_t, pack_u, pack_t2, pack_u2, pack_b, pack_b2, got_t, got_u, got_t2, got_u2, got_b2,
    xb, ub, wall, wdn, pre, dall, scl, pb, sb, fin, x4,
    wsem, xs, xr, zs, zr,
):
    node = lax.axis_index("node")
    loc = lax.axis_index("local")
    y, x = node // 4, node % 4
    z, c = loc // 2, loc % 2

    def xy_dev(q):
        return (((y + q // 4) % 4) * 4 + (x + q % 4) % 4, loc)

    def z_dev(dz):
        return (node, ((z + dz) % 4) * 2 + c)

    sib = (node, z * 2 + 1 - c)

    loads = []
    for e in range(3):
        loads.append(pltpu.make_async_copy(wg.at[e], wall.at[:, pl.ds(256 * e, 128)], wsem.at[3 * e]))
        loads.append(pltpu.make_async_copy(wu.at[e], wall.at[:, pl.ds(256 * e + 128, 128)], wsem.at[3 * e + 1]))
        loads.append(pltpu.make_async_copy(wd.at[e], wdn.at[pl.ds(128 * e, 128), :], wsem.at[3 * e + 2]))

    barrier = pltpu.get_barrier_semaphore()
    for q in range(1, 16):
        pl.semaphore_signal(barrier, inc=1, device_id=xy_dev(q), device_id_type=MESH)
    for peer in (z_dev(1), z_dev(2), z_dev(3), sib):
        pl.semaphore_signal(barrier, inc=1, device_id=peer, device_id_type=MESH)

    started = []

    def start(copy):
        copy.start()
        started.append(copy)

    def remote(k, src, dst, device):
        return pltpu.make_async_remote_copy(
            src_ref=src, dst_ref=dst, send_sem=zs.at[k], recv_sem=zr.at[k],
            device_id=device, device_id_type=MESH,
        )

    def xy_send(k, src, dst):
        copies = [
            pltpu.make_async_remote_copy(
                src_ref=src.at[pl.ds(16 * q, 16), :],
                dst_ref=dst.at[pl.ds(16 * inverse(q), 16), :],
                send_sem=xs.at[k, q],
                recv_sem=xr.at[k, inverse(q)],
                device_id=xy_dev(q),
                device_id_type=MESH,
            )
            for q in NEAR
        ]
        for copy in copies:
            start(copy)
        dst[pl.ds(0, 16), :] = src[pl.ds(0, 16), :]
        return copies

    def arrive(copies):
        for copy in copies:
            copy.wait_recv()

    ui = iota((128, 128), 0)
    uj = iota((128, 128), 1)
    seq_w = seq_weight(seq_ids, ratios)
    rw = (combine_t[...] * seq_w).astype(BF).astype(F32)
    tiled = jnp.dot(
        routes_t[...].astype(F32).astype(BF),
        one_hot((iota((16, 128), 1) & 15) == iota((16, 128), 0)),
        preferred_element_type=F32,
    )
    info[:, pl.ds(256, 128)] = jnp.concatenate([tiled, jnp.zeros((8, 128), F32)], axis=0).astype(BF)
    expert = iota((128, 16), 0)
    same = one_hot(ui == uj)
    for half in range(2):
        acc = jnp.zeros((128, 16), F32)
        for k in range(8):
            acc = acc + jnp.where(routes_t[k : k + 1, :] == expert - 64 * half, rw[k : k + 1, :], 0.0)
        info[:, pl.ds(128 * half, 128)] = lax.dot_general(
            acc.astype(BF), same, TN, preferred_element_type=F32
        ).astype(BF)

    def pack_in(src, mat, dst, notes=None):
        x3[...] = jnp.zeros((128, PW), BF)
        for j in range(3):
            x3[pl.ds(16 * j, 16), :] = src[:, PW * j : PW * (j + 1)]
        for j in range(5):
            x3[pl.ds(48 + 16 * j, 16), pl.ds(128 * j, 128)] = src[:, 3 * PW : D]
        if notes is not None:
            for j in range(5):
                x3[pl.ds(48 + 16 * j, 16), pl.ds(128 * (5 + j // 2), 128)] = notes[:, pl.ds(128 * (j % 2), 128)]
        dst[...] = jnp.dot(mat[...], x3[...], preferred_element_type=F32).astype(BF)

    amat[...] = route_matrix(tiled.astype(I32), y, x)
    pack_in(tok, amat, pack_t, info)

    raw_i = remote(0, info, info2, z_dev(2))
    raw_t = remote(1, tok, tok2, z_dev(2))
    raw_u = remote(2, ups, ups2, z_dev(2))

    pl.semaphore_wait(barrier, 19)
    sent_t = xy_send(0, pack_t, got_t)
    start(raw_i)
    start(raw_t)
    pack_in(ups, amat, pack_u)
    sent_u = xy_send(1, pack_u, got_u)
    start(raw_u)
    for copy in loads:
        copy.start()

    brow = iota((4 * ROWS, 256), 0)
    part = jnp.where(brow >= 80, 1, 0) + jnp.where(brow >= 160, 1, 0) + jnp.where(brow >= 240, 1, 0)
    rem = brow - 80 * part
    bq = (rem * 205) >> 10
    bs = rem - 5 * bq
    bmat[...] = one_hot(iota((4 * ROWS, 256), 1) == bq * 16 + jnp.where(part < 3, 5 * part + bs, 15))
    drow = iota((ROWS, 128), 0)
    dlane = iota((ROWS, 128), 1)
    ds_ = drow - 5 * ((drow * 205) >> 10)
    take = one_hot(((ui & 63) == 3 * node + uj) & (uj < 3))

    raw_i.wait_recv()
    amat2[...] = route_matrix(info2[:, pl.ds(256, 128)].astype(F32).astype(I32), y, x)
    raw_t.wait_recv()
    pack_in(tok2, amat2, pack_t2, info2)

    def unpack(got, dst, place, notes):
        dense = jnp.dot(bmat[...], got[...], preferred_element_type=F32)
        for j in range(3):
            dst[place, pl.ds(PW * j, PW)] = dense[ROWS * j : ROWS * (j + 1), :].astype(BF)
        last = dense[3 * ROWS : 4 * ROWS, :]
        tail = jnp.zeros((ROWS, 128), F32)
        for j in range(5):
            tail = jnp.where(ds_ == j, last[:, 128 * j : 128 * (j + 1)], tail)
        dst[place, pl.ds(3 * PW, 128)] = tail.astype(BF)
        if notes:
            picked = jnp.zeros((ROWS, 128), F32)
            for j in range(5):
                mine = (ds_ == j) & ((dlane >> 6) == j % 2)
                picked = jnp.where(mine, last[:, 128 * (5 + j // 2) : 128 * (6 + j // 2)], picked)
            dst[place, pl.ds(D, 128)] = jnp.dot(picked.astype(BF), take, preferred_element_type=F32).astype(BF)

    def gather_copy(k, buf, src, dst, device):
        return remote(k, buf.at[slot(*src), :], buf.at[slot(*dst), :], device)

    tp = gather_copy(3, xb, (0, 0), (3, 0), z_dev(1))
    tm = gather_copy(4, xb, (0, 0), (1, 0), z_dev(3))
    up = gather_copy(5, ub, (0, 0), (3, 0), z_dev(1))
    um = gather_copy(6, ub, (0, 0), (1, 0), z_dev(3))
    t_sib = {dz: gather_copy(7 + dz, xb, (dz, 0), (dz, 1), sib) for dz in range(4)}
    u_sib = {dz: gather_copy(11 + dz, ub, (dz, 0), (dz, 1), sib) for dz in range(4)}

    arrive(sent_t)
    sent_t2 = xy_send(2, pack_t2, got_t2)
    unpack(got_t, xb, slot(0, 0), True)
    start(tp)
    start(tm)
    start(t_sib[0])

    raw_u.wait_recv()
    pack_in(ups2, amat2, pack_u2)
    arrive(sent_u)
    sent_u2 = xy_send(3, pack_u2, got_u2)
    unpack(got_u, ub, slot(0, 0), False)
    start(up)
    start(um)
    start(u_sib[0])

    def gate_up(r0, m):
        rows = pl.ds(r0, m)
        for e in range(3):
            pre[rows, pl.ds(256 * e, 256)] = jnp.dot(
                xb[rows, pl.ds(0, D)], wall[:, pl.ds(256 * e, 256)], preferred_element_type=F32
            )

    def backward(r0, m):
        rows = pl.ds(r0, m)
        proj_all = lax.dot_general(ub[rows, :], wdn[...], NT, preferred_element_type=F32)
        score = jnp.zeros((m, 128), F32)
        lanes = iota((m, 128), 1)
        for e in range(3):
            gate = pre[rows, pl.ds(256 * e, 128)]
            upv = pre[rows, pl.ds(256 * e + 128, 128)]
            proj = proj_all[:, 128 * e : 128 * (e + 1)]
            scale = xb[rows, pl.ds(D, 128)][:, e : e + 1].astype(F32)
            sig = jax.nn.sigmoid(gate)
            act = gate * sig
            hidden = (act * upv).astype(BF).astype(F32)
            score = jnp.where(lanes == e, jnp.sum(hidden * proj, axis=1, keepdims=True), score)
            dh = scale * proj
            dall[rows, pl.ds(256 * e, 128)] = (dh * upv * sig * (1.0 + gate * (1.0 - sig))).astype(BF)
            dall[rows, pl.ds(256 * e + 128, 128)] = (dh * act).astype(BF)
            scl[rows, pl.ds(128 * e, 128)] = (hidden * scale).astype(BF)
        pb[rows, pl.ds(D, 128)] = score.astype(BF)

        @pl.loop(0, 7)
        def _(i):
            cols = pl.ds(pl.multiple_of(i * 512, 512), 512)
            pb[rows, cols] = lax.dot_general(
                dall[rows, :], wall[cols, :], NT, preferred_element_type=F32
            ).astype(BF)

    p_sib = {
        dz: remote(15 + dz, pb.at[slot(dz, 1), :], sb.at[pl.ds(POS[dz] * ROWS, ROWS), :], sib)
        for dz in range(4)
    }

    def pair_sum(dz):
        p_sib[dz].wait_recv()
        return pb[slot(dz, 0), :].astype(F32) + sb[pl.ds(POS[dz] * ROWS, ROWS), :].astype(F32)

    crow = iota((256, 384), 0)
    clane = iota((256, 384), 1)
    cpart = jnp.where(clane >= 80, 1, 0) + jnp.where(clane >= 160, 1, 0) + jnp.where(clane >= 240, 1, 0)
    crem = clane - 80 * cpart
    cq = (crem * 205) >> 10
    cs = crem - 5 * cq
    cmat[...] = one_hot((crow == cq * 16 + jnp.where(cpart < 3, 5 * cpart + cs, 15)) & (clane < 320))
    x4[...] = jnp.zeros((384, PW), BF)
    repeat = one_hot((ui == (uj & 7)) & (ui < 3))

    def pack_out(total, dst):
        for j in range(3):
            x4[pl.ds(ROWS * j, ROWS), :] = total[:, PW * j : PW * (j + 1)].astype(BF)
        tail = total[:, 3 * PW : D]
        for j in range(5):
            x4[pl.ds(3 * ROWS, ROWS), pl.ds(128 * j, 128)] = jnp.where(ds_ == j, tail, 0.0).astype(BF)
        score = jnp.dot(total[:, D:DT].astype(BF), repeat, preferred_element_type=F32)
        x4[pl.ds(3 * ROWS, ROWS), pl.ds(640, 128)] = jnp.where((dlane >> 3) == ds_, score, 0.0).astype(BF)
        dst[...] = jnp.dot(cmat[...], x4[...], preferred_element_type=F32).astype(BF)

    for copy in loads:
        copy.wait()
    t_sib[0].wait_recv()
    gate_up(0, 160)
    u_sib[0].wait_recv()
    backward(0, 160)
    start(p_sib[0])

    tp.wait_recv()
    start(t_sib[3])
    tm.wait_recv()
    start(t_sib[1])
    arrive(sent_t2)
    unpack(got_t2, xb, slot(2, 0), True)
    start(t_sib[2])
    t_sib[1].wait_recv()
    t_sib[3].wait_recv()
    gate_up(160, 320)
    t_sib[2].wait_recv()
    gate_up(480, 160)
    arrive(sent_u2)
    unpack(got_u2, ub, slot(2, 0), False)
    start(u_sib[2])
    um.wait_recv()
    start(u_sib[1])
    up.wait_recv()
    start(u_sib[3])
    u_sib[2].wait_recv()
    backward(480, 160)
    start(p_sib[2])
    u_sib[1].wait_recv()
    backward(160, 160)
    start(p_sib[1])
    pack_out(pair_sum(2), pack_b2)
    sent_b2 = xy_send(4, pack_b2, got_b2)
    u_sib[3].wait_recv()
    backward(320, 160)
    start(p_sib[3])
    r1 = remote(19, pb.at[slot(1, 0), :], fin.at[0], z_dev(1))
    r3 = remote(20, pb.at[slot(3, 0), :], fin.at[1], z_dev(3))
    pb[slot(1, 0), :] = pair_sum(1).astype(BF)
    start(r1)
    pb[slot(3, 0), :] = pair_sum(3).astype(BF)
    start(r3)

    def weight_grads(first, last):
        @pl.loop(first, last)
        def _(i):
            cols = pl.ds(pl.multiple_of(i * 512, 512), 512)
            grads = lax.dot_general(xb[:, cols], dall[...], TN, preferred_element_type=F32).astype(BF)
            for e in range(3):
                gg[e, cols, :] = grads[:, 256 * e : 256 * e + 128]
                gu[e, cols, :] = grads[:, 256 * e + 128 : 256 * (e + 1)]

    def down_grads(first, last):
        @pl.loop(first, last)
        def _(i):
            cols = pl.ds(pl.multiple_of(i * 512, 512), 512)
            grads = lax.dot_general(scl[...], ub[:, cols], TN, preferred_element_type=F32).astype(BF)
            for e in range(3):
                gd[e, :, cols] = grads[128 * e : 128 * (e + 1), :]

    weight_grads(0, 4)
    arrive(sent_b2)
    parts, tail, score = token_sums(amat2, got_b2, y, x)
    for j in range(3):
        far_out[:, pl.ds(PW * j, PW)] = parts[j].astype(BF)
    far_out[:, pl.ds(3 * PW, 128)] = tail.astype(BF)
    far_out[:, pl.ds(D, 128)] = score.astype(BF)
    raw_b = remote(21, far_out, far, z_dev(2))
    start(raw_b)
    weight_grads(4, 7)

    total = pair_sum(0)
    r1.wait_recv()
    total = total + fin[0].astype(F32)
    r3.wait_recv()
    pack_out(total + fin[1].astype(F32), pack_b)
    sent_b = xy_send(5, pack_b, got_b)
    down_grads(0, 7)
    raw_b.wait_recv()
    arrive(sent_b)
    for copy in started:
        copy.wait_send()


def finish(amat, got_b, far, routes_t, seq_ids, ratios, gg_in, gu_in, gd_in, gt, gc, gg, gu, gd, sems):
    copies = []
    for k, (src, dst) in enumerate(((gg_in, gg), (gu_in, gu), (gd_in, gd))):
        for e in range(3):
            copies.append(pltpu.make_async_copy(src.at[e], dst.at[e], sems.at[3 * k + e]))
    for copy in copies:
        copy.start()
    node = lax.axis_index("node")
    seq_w = seq_weight(seq_ids, ratios)
    parts, tail, score = token_sums(amat, got_b, node // 4, node % 4)
    for j in range(3):
        gt[:, pl.ds(PW * j, PW)] = (parts[j] + far[:, pl.ds(PW * j, PW)].astype(F32)).astype(BF)
    gt[:, pl.ds(3 * PW, 128)] = (tail + far[:, pl.ds(3 * PW, 128)].astype(F32)).astype(BF)
    score = score + far[:, pl.ds(D, 128)].astype(F32)
    eye = one_hot(iota((16, 16), 0) == iota((16, 16), 1))
    scores = lax.dot_general(score.astype(BF), eye, TN, preferred_element_type=F32)
    expert = iota((128, 16), 0)
    for k in range(8):
        value = jnp.sum(jnp.where(routes_t[k : k + 1, :] == expert, scores, 0.0), axis=0, keepdims=True)
        gc[pl.ds(k, 1), :] = value * seq_w[k : k + 1, :]
    for copy in copies:
        copy.wait()


def local(tokens, upstream, routes, combine, seq_ids, ratios, w_gate, w_up, w_down):
    vmem = pl.BlockSpec(memory_space=pltpu.VMEM)
    hbm = pl.BlockSpec(memory_space=pl.ANY)
    shape = jax.ShapeDtypeStruct
    dma = pltpu.SemaphoreType.DMA
    routes_t, combine_t, seq_ids, ratios = routes.T, combine.T, seq_ids[None, :], ratios[None, :]
    amat, got_b, far, *grads = pl.pallas_call(
        kernel,
        out_shape=(
            pltpu.VMEM((256, 128), BF),
            pltpu.VMEM((256, PW), BF),
            pltpu.VMEM((16, DT), BF),
            pltpu.VMEM((3, D, 128), BF),
            pltpu.VMEM((3, D, 128), BF),
            pltpu.VMEM((3, 128, D), BF),
        ),
        in_specs=[vmem] * 6 + [hbm] * 3,
        out_specs=(vmem,) * 6,
        scratch_shapes=[
            pltpu.VMEM((256, 128), BF),
            pltpu.VMEM((320, 256), BF),
            pltpu.VMEM((256, 384), BF),
            pltpu.VMEM((128, PW), BF),
            pltpu.VMEM((16, 384), BF),
            pltpu.VMEM((16, D), BF),
            pltpu.VMEM((16, D), BF),
            pltpu.VMEM((16, 384), BF),
            pltpu.VMEM((16, DT), BF),
        ]
        + [pltpu.VMEM((256, PW), BF)] * 11
        + [
            pltpu.VMEM((640, DT), BF),
            pltpu.VMEM((640, D), BF),
            pltpu.VMEM((D, 768), BF),
            pltpu.VMEM((384, D), BF),
            pltpu.VMEM((640, 768), F32),
            pltpu.VMEM((640, 768), BF),
            pltpu.VMEM((640, 384), BF),
            pltpu.VMEM((640, DT), BF),
            pltpu.VMEM((320, DT), BF),
            pltpu.VMEM((2, ROWS, DT), BF),
            pltpu.VMEM((384, PW), BF),
            dma((9,)), dma((6, 16)), dma((6, 16)), dma((22,)), dma((22,)),
        ],
        compiler_params=pltpu.CompilerParams(
            collective_id=0, has_side_effects=True, vmem_limit_bytes=46 << 20
        ),
        name="moe_grad",
    )(tokens, upstream, routes_t, combine_t, seq_ids, ratios, w_gate, w_up, w_down)
    gt, gc, gg, gu, gd = pl.pallas_call(
        finish,
        out_shape=(
            shape((16, D), BF),
            shape((8, 16), F32),
            shape((3, D, 128), BF),
            shape((3, D, 128), BF),
            shape((3, 128, D), BF),
        ),
        in_specs=[vmem] * 9,
        out_specs=(vmem, vmem, hbm, hbm, hbm),
        scratch_shapes=[dma((9,))],
        compiler_params=pltpu.CompilerParams(vmem_limit_bytes=16 << 20),
        name="moe_finish",
    )(amat, got_b, far, routes_t, seq_ids, ratios, *grads)
    return gt, gc.T, gg, gu, gd


def solution(mesh):
    rows = P(("node", "local"), None)
    return jax.shard_map(
        local,
        mesh=mesh,
        in_specs=(
            rows, rows, rows, rows, P(("node", "local")), P(),
            P("node", None, "local"), P("node", None, "local"), P("node", "local", None),
        ),
        out_specs=(rows, rows, P("node", None, "local"), P("node", None, "local"), P("node", "local", None)),
        check_vma=False,
    )
```

time: 104 us -> 92.5 us (0.89)
  Pallas kernels: 104 us -> 91.5 us
    pallas_call x1, Pallas kernels: 99.3 us -> 87.4 us  [local(): pl.pallas_call(kernel, out_shape=(pltpu.VMEM((256, 128), BF), pltpu.VMEM(...]
where the time goes in v3:
time: 92.5 us; the launch traced here: 92.4 us
  Pallas kernels  91.5 us (99%)
    pallas_call x1, Pallas kernels, local(): pl.pallas_call(kernel, out_shape=(pltpu.VMEM((256, 128), BF), pltpu.VMEM(...  87.4 us
    pallas_call x1, Pallas kernels, local(): pl.pallas_call(finish, out_shape=(shape((16, D), BF), shape((8, 16), F32)...  4.08 us

profile of v3, /device:TPU:1, one launch (start us, length us, event | category | flops | bytes accessed | tf_op | source)
XLA Modules:
  0.0 92.4 jit_solution(7898780456611996751)
XLA Ops:
  0.6 0.0 copy-start
  0.6 0.0 copy-start.1
  0.7 0.0 copy-start.2
  0.7 87.4 %moe_grad.1 = (bf16[256,128]{1,0:T(8,128)(2,1)S(1)}, bf16[256,1152]{1,0:T(8,128)(2,1)S(1)}, bf16[16,3712]{1,0:T(8,128)(2,1)S(1)}, bf16[3,3584,128]{2,1,0:T(8,128...) custom-call(bf16[16,3584]{1,0:T(8,128)(2,1)} %tok.1, bf16[16,3584]{1,0:T(8,128)(2,1)} %ups.1, ...), custom_call_target="tpu_custom_call" | custom-call | tf_op jit(solution)/shard_map/moe_grad/pallas_call | solution.py:441
  88.1 0.0 copy-done
  88.1 0.0 copy-done.1
  88.1 0.0 copy-done.2
  88.1 4.1 %moe_finish.1 = (bf16[16,3584]{1,0:T(8,128)(2,1)}, f32[8,16]{1,0:T(8,128)}, bf16[3,3584,128]{2,1,0:T(8,128)(2,1)}, bf16[3,3584,128]{2,1,0:T(8,128)(2,1)}, bf16[3,128,3584]{2,1,0:T(8,128)(2,1)}) custom-call(bf16[256,128]{1,0:T(8,128)(2,1)S(1)} %get-tuple-element.16.amat, bf16[256,1152]{1,0:T(8,128)(2,1)S(1)} %get-tuple-element.17.got_b, ...), custom_call_target="tpu_custom_call" | custom-call | tf_op jit(solution)/shard_map/moe_finish/pallas_call | solution.py:484
Async XLA Ops:
  0.6 87.4 %copy-start = (s32[16,8]{0,1:T(8,128)S(1)}, s32[16,8]{0,1:T(8,128)}, u32[]{:S(2)}) copy-start(s32[16,8]{0,1:T(8,128)} %param.11) | copy-start | bytes 1540
  0.6 87.4 %copy-start.1 = (f32[256]{0:T(256)S(1)}, f32[256]{0:T(256)}, u32[]{:S(2)}) copy-start(f32[256]{0:T(256)} %param.14) | copy-start | bytes 3076
  0.7 87.4 %copy-start.2 = (s32[16]{0:T(128)S(1)}, s32[16]{0:T(128)}, u32[]{:S(2)}) copy-start(s32[16]{0:T(128)} %param.13) | copy-start | bytes 196

commit v4 on v3

--- a/solution.py
+++ b/solution.py
@@ -16,12 +16,18 @@
 ROWS = 80
 POS = {0: 0, 1: 1, 3: 2, 2: 3}
 NEAR = (1, 3, 4, 12, 2, 5, 7, 8, 13, 15, 6, 9, 11, 14, 10)
+PIECES = ((0, 640), (640, 512))
 NT = (((1,), (1,)), ((), ()))
 TN = (((0,), (0,)), ((), ()))
 
 
 def slot(dz, dc):
     return pl.ds((POS[dz] * 2 + dc) * ROWS, ROWS)
+
+
+def dense_slices(p):
+    first, width = PIECES[p]
+    return [pl.ds(PW * j + first, width) for j in range(3)] + [pl.ds(3 * PW + 128 * p, 128)]
 
 
 def inverse(q):
@@ -126,17 +132,22 @@
         copy.start()
         started.append(copy)
 
-    def remote(k, src, dst, device):
+    used = []
+
+    def remote(src, dst, device):
+        k = len(used)
+        used.append(k)
         return pltpu.make_async_remote_copy(
             src_ref=src, dst_ref=dst, send_sem=zs.at[k], recv_sem=zr.at[k],
             device_id=device, device_id_type=MESH,
         )
 
-    def xy_send(k, src, dst):
+    def xy_send(k, src, dst, first=0, width=PW):
+        cols = pl.ds(first, width)
         copies = [
             pltpu.make_async_remote_copy(
-                src_ref=src.at[pl.ds(16 * q, 16), :],
-                dst_ref=dst.at[pl.ds(16 * inverse(q), 16), :],
+                src_ref=src.at[pl.ds(16 * q, 16), cols],
+                dst_ref=dst.at[pl.ds(16 * inverse(q), 16), cols],
                 send_sem=xs.at[k, q],
                 recv_sem=xr.at[k, inverse(q)],
                 device_id=xy_dev(q),
@@ -146,7 +157,7 @@
         ]
         for copy in copies:
             start(copy)
-        dst[pl.ds(0, 16), :] = src[pl.ds(0, 16), :]
+        dst[pl.ds(0, 16), cols] = src[pl.ds(0, 16), cols]
         return copies
 
     def arrive(copies):
@@ -155,13 +166,40 @@
 
     ui = iota((128, 128), 0)
     uj = iota((128, 128), 1)
-    seq_w = seq_weight(seq_ids, ratios)
-    rw = (combine_t[...] * seq_w).astype(BF).astype(F32)
+
+    def pack_rows(src):
+        x3[...] = jnp.zeros((128, PW), BF)
+        for j in range(3):
+            x3[pl.ds(16 * j, 16), :] = src[:, PW * j : PW * (j + 1)]
+        for j in range(5):
+            x3[pl.ds(48 + 16 * j, 16), pl.ds(128 * j, 128)] = src[:, 3 * PW : D]
+
+    def pack_notes(notes):
+        for j in range(5):
+            x3[pl.ds(48 + 16 * j, 16), pl.ds(128 * (5 + j // 2), 128)] = notes[:, pl.ds(128 * (j % 2), 128)]
+
+    def pack_in(mat, dst, first=0, width=PW):
+        cols = pl.ds(first, width)
+        dst[:, cols] = jnp.dot(mat[...], x3[:, cols], preferred_element_type=F32).astype(BF)
+
     tiled = jnp.dot(
         routes_t[...].astype(F32).astype(BF),
         one_hot((iota((16, 128), 1) & 15) == iota((16, 128), 0)),
         preferred_element_type=F32,
     )
+    amat[...] = route_matrix(tiled.astype(I32), y, x)
+    pack_rows(tok)
+    pack_in(amat, pack_t, *PIECES[0])
+
+    raw_i = remote(info, info2, z_dev(2))
+    raw_t = remote(tok, tok2, z_dev(2))
+    raw_u = remote(ups, ups2, z_dev(2))
+
+    pl.semaphore_wait(barrier, 19)
+    sent_t = [xy_send(0, pack_t, got_t, *PIECES[0])]
+
+    seq_w = seq_weight(seq_ids, ratios)
+    rw = (combine_t[...] * seq_w).astype(BF).astype(F32)
     info[:, pl.ds(256, 128)] = jnp.concatenate([tiled, jnp.zeros((8, 128), F32)], axis=0).astype(BF)
     expert = iota((128, 16), 0)
     same = one_hot(ui == uj)
@@ -172,32 +210,15 @@
         info[:, pl.ds(128 * half, 128)] = lax.dot_general(
             acc.astype(BF), same, TN, preferred_element_type=F32
         ).astype(BF)
-
-    def pack_in(src, mat, dst, notes=None):
-        x3[...] = jnp.zeros((128, PW), BF)
-        for j in range(3):
-            x3[pl.ds(16 * j, 16), :] = src[:, PW * j : PW * (j + 1)]
-        for j in range(5):
-            x3[pl.ds(48 + 16 * j, 16), pl.ds(128 * j, 128)] = src[:, 3 * PW : D]
-        if notes is not None:
-            for j in range(5):
-                x3[pl.ds(48 + 16 * j, 16), pl.ds(128 * (5 + j // 2), 128)] = notes[:, pl.ds(128 * (j % 2), 128)]
-        dst[...] = jnp.dot(mat[...], x3[...], preferred_element_type=F32).astype(BF)
-
-    amat[...] = route_matrix(tiled.astype(I32), y, x)
-    pack_in(tok, amat, pack_t, info)
-
-    raw_i = remote(0, info, info2, z_dev(2))
-    raw_t = remote(1, tok, tok2, z_dev(2))
-    raw_u = remote(2, ups, ups2, z_dev(2))
-
-    pl.semaphore_wait(barrier, 19)
-    sent_t = xy_send(0, pack_t, got_t)
+    pack_notes(info)
+    pack_in(amat, pack_t, *PIECES[1])
+    sent_t.append(xy_send(6, pack_t, got_t, *PIECES[1]))
     start(raw_i)
     start(raw_t)
-    pack_in(ups, amat, pack_u)
+    start(raw_u)
+    pack_rows(ups)
+    pack_in(amat, pack_u)
     sent_u = xy_send(1, pack_u, got_u)
-    start(raw_u)
     for copy in loads:
         copy.start()
 
@@ -212,49 +233,59 @@
     ds_ = drow - 5 * ((drow * 205) >> 10)
     take = one_hot(((ui & 63) == 3 * node + uj) & (uj < 3))
 
+    def unpack(p, got, dst, place, notes=False):
+        first, width = PIECES[p]
+        dense = jnp.dot(bmat[...], got[:, pl.ds(first, width)], preferred_element_type=F32)
+        for j in range(3):
+            dst[place, pl.ds(PW * j + first, width)] = dense[ROWS * j : ROWS * (j + 1), :].astype(BF)
+        last = dense[3 * ROWS : 4 * ROWS, :]
+        if p == 0:
+            tail = jnp.zeros((ROWS, 128), F32)
+            for j in range(5):
+                tail = jnp.where(ds_ == j, last[:, 128 * j : 128 * (j + 1)], tail)
+            dst[place, pl.ds(3 * PW, 128)] = tail.astype(BF)
+        elif notes:
+            picked = jnp.zeros((ROWS, 128), F32)
+            for j in range(5):
+                mine = (ds_ == j) & ((dlane >> 6) == j % 2)
+                picked = jnp.where(mine, last[:, 128 * (j // 2) : 128 * (1 + j // 2)], picked)
+            dst[place, pl.ds(D, 128)] = jnp.dot(picked.astype(BF), take, preferred_element_type=F32).astype(BF)
+
+    def gather_copy(buf, src, dst, device):
+        return remote(buf.at[slot(*src), :], buf.at[slot(*dst), :], device)
+
+    def pieces(src, dst, device):
+        return [[remote(src(cols), dst(cols), device) for cols in dense_slices(p)] for p in range(2)]
+
+    tp = pieces(lambda cols: xb.at[slot(0, 0), cols], lambda cols: xb.at[slot(3, 0), cols], z_dev(1))
+    tm = pieces(lambda cols: xb.at[slot(0, 0), cols], lambda cols: xb.at[slot(1, 0), cols], z_dev(3))
+    up = gather_copy(ub, (0, 0), (3, 0), z_dev(1))
+    um = gather_copy(ub, (0, 0), (1, 0), z_dev(3))
+    t_sib = {dz: gather_copy(xb, (dz, 0), (dz, 1), sib) for dz in range(4)}
+    u_sib = {dz: gather_copy(ub, (dz, 0), (dz, 1), sib) for dz in range(4)}
+
+    for p in range(2):
+        arrive(sent_t[p])
+        unpack(p, got_t, xb, slot(0, 0), True)
+        for plus, minus in zip(tp[p], tm[p]):
+            start(plus)
+            start(minus)
+    start(t_sib[0])
+
     raw_i.wait_recv()
     amat2[...] = route_matrix(info2[:, pl.ds(256, 128)].astype(F32).astype(I32), y, x)
     raw_t.wait_recv()
-    pack_in(tok2, amat2, pack_t2, info2)
-
-    def unpack(got, dst, place, notes):
-        dense = jnp.dot(bmat[...], got[...], preferred_element_type=F32)
-        for j in range(3):
-            dst[place, pl.ds(PW * j, PW)] = dense[ROWS * j : ROWS * (j + 1), :].astype(BF)
-        last = dense[3 * ROWS : 4 * ROWS, :]
-        tail = jnp.zeros((ROWS, 128), F32)
-        for j in range(5):
-            tail = jnp.where(ds_ == j, last[:, 128 * j : 128 * (j + 1)], tail)
-        dst[place, pl.ds(3 * PW, 128)] = tail.astype(BF)
-        if notes:
-            picked = jnp.zeros((ROWS, 128), F32)
-            for j in range(5):
-                mine = (ds_ == j) & ((dlane >> 6) == j % 2)
-                picked = jnp.where(mine, last[:, 128 * (5 + j // 2) : 128 * (6 + j // 2)], picked)
-            dst[place, pl.ds(D, 128)] = jnp.dot(picked.astype(BF), take, preferred_element_type=F32).astype(BF)
-
-    def gather_copy(k, buf, src, dst, device):
-        return remote(k, buf.at[slot(*src), :], buf.at[slot(*dst), :], device)
-
-    tp = gather_copy(3, xb, (0, 0), (3, 0), z_dev(1))
-    tm = gather_copy(4, xb, (0, 0), (1, 0), z_dev(3))
-    up = gather_copy(5, ub, (0, 0), (3, 0), z_dev(1))
-    um = gather_copy(6, ub, (0, 0), (1, 0), z_dev(3))
-    t_sib = {dz: gather_copy(7 + dz, xb, (dz, 0), (dz, 1), sib) for dz in range(4)}
-    u_sib = {dz: gather_copy(11 + dz, ub, (dz, 0), (dz, 1), sib) for dz in range(4)}
-
-    arrive(sent_t)
+    pack_rows(tok2)
+    pack_notes(info2)
+    pack_in(amat2, pack_t2)
     sent_t2 = xy_send(2, pack_t2, got_t2)
-    unpack(got_t, xb, slot(0, 0), True)
-    start(tp)
-    start(tm)
-    start(t_sib[0])
-
     raw_u.wait_recv()
-    pack_in(ups2, amat2, pack_u2)
+    pack_rows(ups2)
+    pack_in(amat2, pack_u2)
     arrive(sent_u)
     sent_u2 = xy_send(3, pack_u2, got_u2)
-    unpack(got_u, ub, slot(0, 0), False)
+    for p in range(2):
+        unpack(p, got_u, ub, slot(0, 0))
     start(up)
     start(um)
     start(u_sib[0])
@@ -294,13 +325,12 @@
             ).astype(BF)
 
     p_sib = {
-        dz: remote(15 + dz, pb.at[slot(dz, 1), :], sb.at[pl.ds(POS[dz] * ROWS, ROWS), :], sib)
+        dz: remote(pb.at[slot(dz, 1), :], sb.at[pl.ds(POS[dz] * ROWS, ROWS), :], sib)
         for dz in range(4)
     }
 
-    def pair_sum(dz):
-        p_sib[dz].wait_recv()
-        return pb[slot(dz, 0), :].astype(F32) + sb[pl.ds(POS[dz] * ROWS, ROWS), :].astype(F32)
+    def pair_sum(dz, cols):
+        return pb[slot(dz, 0), cols].astype(F32) + sb[pl.ds(POS[dz] * ROWS, ROWS), cols].astype(F32)
 
     crow = iota((256, 384), 0)
     clane = iota((256, 384), 1)
@@ -312,15 +342,21 @@
     x4[...] = jnp.zeros((384, PW), BF)
     repeat = one_hot((ui == (uj & 7)) & (ui < 3))
 
-    def pack_out(total, dst):
+    def pack_out(p, total, dst):
+        first, width = PIECES[p]
+        slices = dense_slices(p)
         for j in range(3):
-            x4[pl.ds(ROWS * j, ROWS), :] = total[:, PW * j : PW * (j + 1)].astype(BF)
-        tail = total[:, 3 * PW : D]
-        for j in range(5):
-            x4[pl.ds(3 * ROWS, ROWS), pl.ds(128 * j, 128)] = jnp.where(ds_ == j, tail, 0.0).astype(BF)
-        score = jnp.dot(total[:, D:DT].astype(BF), repeat, preferred_element_type=F32)
-        x4[pl.ds(3 * ROWS, ROWS), pl.ds(640, 128)] = jnp.where((dlane >> 3) == ds_, score, 0.0).astype(BF)
-        dst[...] = jnp.dot(cmat[...], x4[...], preferred_element_type=F32).astype(BF)
+            x4[pl.ds(ROWS * j, ROWS), pl.ds(first, width)] = total(slices[j]).astype(BF)
+        extra = total(slices[3])
+        if p == 0:
+            for j in range(5):
+                x4[pl.ds(3 * ROWS, ROWS), pl.ds(128 * j, 128)] = jnp.where(ds_ == j, extra, 0.0).astype(BF)
+        else:
+            score = jnp.dot(extra.astype(BF), repeat, preferred_element_type=F32)
+            x4[pl.ds(3 * ROWS, ROWS), pl.ds(640, 128)] = jnp.where((dlane >> 3) == ds_, score, 0.0).astype(BF)
+        dst[:, pl.ds(first, width)] = jnp.dot(
+            cmat[...], x4[:, pl.ds(first, width)], preferred_element_type=F32
+        ).astype(BF)
 
     for copy in loads:
         copy.wait()
@@ -330,12 +366,13 @@
     backward(0, 160)
     start(p_sib[0])
 
-    tp.wait_recv()
+    arrive(tp[0] + tp[1])
     start(t_sib[3])
-    tm.wait_recv()
+    arrive(tm[0] + tm[1])
     start(t_sib[1])
     arrive(sent_t2)
-    unpack(got_t2, xb, slot(2, 0), True)
+    for p in range(2):
+        unpack(p, got_t2, xb, slot(2, 0), True)
     start(t_sib[2])
     t_sib[1].wait_recv()
     t_sib[3].wait_recv()
@@ -343,7 +380,8 @@
     t_sib[2].wait_recv()
     gate_up(480, 160)
     arrive(sent_u2)
-    unpack(got_u2, ub, slot(2, 0), False)
+    for p in range(2):
+        unpack(p, got_u2, ub, slot(2, 0))
     start(u_sib[2])
     um.wait_recv()
     start(u_sib[1])
@@ -353,19 +391,26 @@
     backward(480, 160)
     start(p_sib[2])
     u_sib[1].wait_recv()
-    backward(160, 160)
+    u_sib[3].wait_recv()
+    backward(160, 320)
     start(p_sib[1])
-    pack_out(pair_sum(2), pack_b2)
+    start(p_sib[3])
+    r1 = pieces(lambda cols: pb.at[slot(1, 0), cols], lambda cols: fin.at[0, :, cols], z_dev(1))
+    r3 = pieces(lambda cols: pb.at[slot(3, 0), cols], lambda cols: fin.at[1, :, cols], z_dev(3))
+
+    def reduce_send(p):
+        for dz, copies in ((1, r1), (3, r3)):
+            for cols, copy in zip(dense_slices(p), copies[p]):
+                pb[slot(dz, 0), cols] = pair_sum(dz, cols).astype(BF)
+                start(copy)
+
+    p_sib[1].wait_recv()
+    p_sib[3].wait_recv()
+    reduce_send(0)
+    p_sib[2].wait_recv()
+    for p in range(2):
+        pack_out(p, lambda cols: pair_sum(2, cols), pack_b2)
     sent_b2 = xy_send(4, pack_b2, got_b2)
-    u_sib[3].wait_recv()
-    backward(320, 160)
-    start(p_sib[3])
-    r1 = remote(19, pb.at[slot(1, 0), :], fin.at[0], z_dev(1))
-    r3 = remote(20, pb.at[slot(3, 0), :], fin.at[1], z_dev(3))
-    pb[slot(1, 0), :] = pair_sum(1).astype(BF)
-    start(r1)
-    pb[slot(3, 0), :] = pair_sum(3).astype(BF)
-    start(r3)
 
     def weight_grads(first, last):
         @pl.loop(first, last)
@@ -384,26 +429,31 @@
             for e in range(3):
                 gd[e, :, cols] = grads[128 * e : 128 * (e + 1), :]
 
-    weight_grads(0, 4)
+    weight_grads(0, 2)
+    reduce_send(1)
+    weight_grads(2, 5)
     arrive(sent_b2)
     parts, tail, score = token_sums(amat2, got_b2, y, x)
     for j in range(3):
         far_out[:, pl.ds(PW * j, PW)] = parts[j].astype(BF)
     far_out[:, pl.ds(3 * PW, 128)] = tail.astype(BF)
     far_out[:, pl.ds(D, 128)] = score.astype(BF)
-    raw_b = remote(21, far_out, far, z_dev(2))
+    raw_b = remote(far_out, far, z_dev(2))
     start(raw_b)
-    weight_grads(4, 7)
-
-    total = pair_sum(0)
-    r1.wait_recv()
-    total = total + fin[0].astype(F32)
-    r3.wait_recv()
-    pack_out(total + fin[1].astype(F32), pack_b)
-    sent_b = xy_send(5, pack_b, got_b)
+    p_sib[0].wait_recv()
+    sent_b = []
+    for p in range(2):
+        arrive(r1[p] + r3[p])
+        pack_out(
+            p, lambda cols: pair_sum(0, cols) + fin[0, :, cols].astype(F32) + fin[1, :, cols].astype(F32), pack_b
+        )
+        sent_b.append(xy_send(5 + 2 * p, pack_b, got_b, *PIECES[p]))
+        if p == 0:
+            weight_grads(5, 7)
     down_grads(0, 7)
     raw_b.wait_recv()
-    arrive(sent_b)
+    for p in range(2):
+        arrive(sent_b[p])
     for copy in started:
         copy.wait_send()
 
@@ -474,7 +524,7 @@
             pltpu.VMEM((320, DT), BF),
             pltpu.VMEM((2, ROWS, DT), BF),
             pltpu.VMEM((384, PW), BF),
-            dma((9,)), dma((6, 16)), dma((6, 16)), dma((22,)), dma((22,)),
+            dma((9,)), dma((8, 16)), dma((8, 16)), dma((64,)), dma((64,)),
         ],
         compiler_params=pltpu.CompilerParams(
             collective_id=0, has_side_effects=True, vmem_limit_bytes=46 << 20

time: 92.5 us -> 85.1 us (0.920)
  Pallas kernels: 91.5 us -> 83.2 us
    pallas_call x1, Pallas kernels: 87.4 us -> 79.1 us  [local(): pl.pallas_call(kernel, out_shape=(pltpu.VMEM((256, 128), BF), pltpu.VMEM(...]
where the time goes in v4:
time: 85.1 us; the launch traced here: 84.1 us
  Pallas kernels  83.2 us (98%)
    pallas_call x1, Pallas kernels, local(): pl.pallas_call(kernel, out_shape=(pltpu.VMEM((256, 128), BF), pltpu.VMEM(...  79.1 us
    pallas_call x1, Pallas kernels, local(): pl.pallas_call(finish, out_shape=(shape((16, D), BF), shape((8, 16), F32)...  4.08 us

profile of v4, /device:TPU:1, one launch (start us, length us, event | category | flops | bytes accessed | tf_op | source)
XLA Modules:
  0.0 84.1 jit_solution(18317248232542119557)
XLA Ops:
  0.6 0.0 copy-start
  0.6 0.0 copy-start.1
  0.7 0.0 copy-start.2
  0.7 79.1 %moe_grad.1 = (bf16[256,128]{1,0:T(8,128)(2,1)S(1)}, bf16[256,1152]{1,0:T(8,128)(2,1)S(1)}, bf16[16,3712]{1,0:T(8,128)(2,1)S(1)}, bf16[3,3584,128]{2,1,0:T(8,128...) custom-call(bf16[16,3584]{1,0:T(8,128)(2,1)} %tok.1, bf16[16,3584]{1,0:T(8,128)(2,1)} %ups.1, ...), custom_call_target="tpu_custom_call" | custom-call | tf_op jit(solution)/shard_map/moe_grad/pallas_call | solution.py:491
  79.8 0.0 copy-done
  79.8 0.0 copy-done.1
  79.8 0.0 copy-done.2
  79.8 4.1 %moe_finish.1 = (bf16[16,3584]{1,0:T(8,128)(2,1)}, f32[8,16]{1,0:T(8,128)}, bf16[3,3584,128]{2,1,0:T(8,128)(2,1)}, bf16[3,3584,128]{2,1,0:T(8,128)(2,1)}, bf16[3,128,3584]{2,1,0:T(8,128)(2,1)}) custom-call(bf16[256,128]{1,0:T(8,128)(2,1)S(1)} %get-tuple-element.16.amat, bf16[256,1152]{1,0:T(8,128)(2,1)S(1)} %get-tuple-element.17.got_b, ...), custom_call_target="tpu_custom_call" | custom-call | tf_op jit(solution)/shard_map/moe_finish/pallas_call | solution.py:534
Async XLA Ops:
  0.6 79.2 %copy-start = (s32[16,8]{0,1:T(8,128)S(1)}, s32[16,8]{0,1:T(8,128)}, u32[]{:S(2)}) copy-start(s32[16,8]{0,1:T(8,128)} %param.11) | copy-start | bytes 1540
  0.6 79.2 %copy-start.1 = (f32[256]{0:T(256)S(1)}, f32[256]{0:T(256)}, u32[]{:S(2)}) copy-start(f32[256]{0:T(256)} %param.14) | copy-start | bytes 3076
  0.7 79.2 %copy-start.2 = (s32[16]{0:T(128)S(1)}, s32[16]{0:T(128)}, u32[]{:S(2)}) copy-start(s32[16]{0:T(128)} %param.13) | copy-start | bytes 196

commit v5 on v4

--- a/solution.py
+++ b/solution.py
@@ -12,6 +12,7 @@
 
 D = 3584
 DT = D + 128
+CA = 1792
 PW = 1152
 ROWS = 80
 POS = {0: 0, 1: 1, 3: 2, 2: 3}
@@ -259,10 +260,17 @@
 
     tp = pieces(lambda cols: xb.at[slot(0, 0), cols], lambda cols: xb.at[slot(3, 0), cols], z_dev(1))
     tm = pieces(lambda cols: xb.at[slot(0, 0), cols], lambda cols: xb.at[slot(1, 0), cols], z_dev(3))
-    up = gather_copy(ub, (0, 0), (3, 0), z_dev(1))
-    um = gather_copy(ub, (0, 0), (1, 0), z_dev(3))
+    def half_copies(src, dst, device):
+        return [remote(src(cols), dst(cols), device) for cols in (pl.ds(0, CA), pl.ds(CA, D - CA))]
+
+    up = half_copies(lambda cols: ub.at[slot(0, 0), cols], lambda cols: ub.at[slot(3, 0), cols], z_dev(1))
+    um = half_copies(lambda cols: ub.at[slot(0, 0), cols], lambda cols: ub.at[slot(1, 0), cols], z_dev(3))
     t_sib = {dz: gather_copy(xb, (dz, 0), (dz, 1), sib) for dz in range(4)}
-    u_sib = {dz: gather_copy(ub, (dz, 0), (dz, 1), sib) for dz in range(4)}
+    u_sib = {dz: gather_copy(ub, (dz, 0), (dz, 1), sib) for dz in (0, 2)}
+    for dz in (1, 3):
+        u_sib[dz] = half_copies(
+            lambda cols, dz=dz: ub.at[slot(dz, 0), cols], lambda cols, dz=dz: ub.at[slot(dz, 1), cols], sib
+        )
 
     for p in range(2):
         arrive(sent_t[p])
@@ -286,8 +294,9 @@
     sent_u2 = xy_send(3, pack_u2, got_u2)
     for p in range(2):
         unpack(p, got_u, ub, slot(0, 0))
-    start(up)
-    start(um)
+    for h in range(2):
+        start(up[h])
+        start(um[h])
     start(u_sib[0])
 
     def gate_up(r0, m):
@@ -297,7 +306,7 @@
                 xb[rows, pl.ds(0, D)], wall[:, pl.ds(256 * e, 256)], preferred_element_type=F32
             )
 
-    def backward(r0, m):
+    def backward(r0, m, chips):
         rows = pl.ds(r0, m)
         proj_all = lax.dot_general(ub[rows, :], wdn[...], NT, preferred_element_type=F32)
         score = jnp.zeros((m, 128), F32)
@@ -317,15 +326,26 @@
             scl[rows, pl.ds(128 * e, 128)] = (hidden * scale).astype(BF)
         pb[rows, pl.ds(D, 128)] = score.astype(BF)
 
-        @pl.loop(0, 7)
-        def _(i):
-            cols = pl.ds(pl.multiple_of(i * 512, 512), 512)
-            pb[rows, cols] = lax.dot_general(
-                dall[rows, :], wall[cols, :], NT, preferred_element_type=F32
-            ).astype(BF)
+        def partial(first, last):
+            @pl.loop(first, last)
+            def _(i):
+                cols = pl.ds(pl.multiple_of(i * 512, 512), 512)
+                pb[rows, cols] = lax.dot_general(
+                    dall[rows, :], wall[cols, :], NT, preferred_element_type=F32
+                ).astype(BF)
+
+        partial(0, 4)
+        for dz in chips:
+            start(p_sib[dz][0])
+        partial(4, 7)
+        for dz in chips:
+            start(p_sib[dz][1])
 
     p_sib = {
-        dz: remote(pb.at[slot(dz, 1), :], sb.at[pl.ds(POS[dz] * ROWS, ROWS), :], sib)
+        dz: [
+            remote(pb.at[slot(dz, 1), cols], sb.at[pl.ds(POS[dz] * ROWS, ROWS), cols], sib)
+            for cols in (pl.ds(0, 2048), pl.ds(2048, DT - 2048))
+        ]
         for dz in range(4)
     }
 
@@ -362,9 +382,6 @@
         copy.wait()
     t_sib[0].wait_recv()
     gate_up(0, 160)
-    u_sib[0].wait_recv()
-    backward(0, 160)
-    start(p_sib[0])
 
     arrive(tp[0] + tp[1])
     start(t_sib[3])
@@ -383,18 +400,15 @@
     for p in range(2):
         unpack(p, got_u2, ub, slot(2, 0))
     start(u_sib[2])
-    um.wait_recv()
-    start(u_sib[1])
-    up.wait_recv()
-    start(u_sib[3])
+    for h in range(2):
+        um[h].wait_recv()
+        start(u_sib[1][h])
+        up[h].wait_recv()
+        start(u_sib[3][h])
     u_sib[2].wait_recv()
-    backward(480, 160)
-    start(p_sib[2])
-    u_sib[1].wait_recv()
-    u_sib[3].wait_recv()
-    backward(160, 320)
-    start(p_sib[1])
-    start(p_sib[3])
+    backward(480, 160, (2,))
+    arrive(u_sib[1] + u_sib[3])
+    backward(160, 320, (1, 3))
     r1 = pieces(lambda cols: pb.at[slot(1, 0), cols], lambda cols: fin.at[0, :, cols], z_dev(1))
     r3 = pieces(lambda cols: pb.at[slot(3, 0), cols], lambda cols: fin.at[1, :, cols], z_dev(3))
 
@@ -404,10 +418,9 @@
                 pb[slot(dz, 0), cols] = pair_sum(dz, cols).astype(BF)
                 start(copy)
 
-    p_sib[1].wait_recv()
-    p_sib[3].wait_recv()
+    arrive(p_sib[1] + p_sib[3])
     reduce_send(0)
-    p_sib[2].wait_recv()
+    arrive(p_sib[2])
     for p in range(2):
         pack_out(p, lambda cols: pair_sum(2, cols), pack_b2)
     sent_b2 = xy_send(4, pack_b2, got_b2)
@@ -429,8 +442,11 @@
             for e in range(3):
                 gd[e, :, cols] = grads[128 * e : 128 * (e + 1), :]
 
-    weight_grads(0, 2)
+    u_sib[0].wait_recv()
+    backward(0, 160, (0,))
+    weight_grads(0, 1)
     reduce_send(1)
+    weight_grads(1, 2)
     weight_grads(2, 5)
     arrive(sent_b2)
     parts, tail, score = token_sums(amat2, got_b2, y, x)
@@ -440,7 +456,7 @@
     far_out[:, pl.ds(D, 128)] = score.astype(BF)
     raw_b = remote(far_out, far, z_dev(2))
     start(raw_b)
-    p_sib[0].wait_recv()
+    arrive(p_sib[0])
     sent_b = []
     for p in range(2):
         arrive(r1[p] + r3[p])

time: 85.1 us -> 83.7 us (0.984); the launches traced: 84.1 us -> 83.5 us
  no operation moved by 1% of the time
where the time goes in v5:
time: 83.7 us; the launch traced here: 83.5 us
  Pallas kernels  82.7 us (99%)
  between operations  0.85 us (1%)
    pallas_call x1, Pallas kernels, local(): pl.pallas_call(kernel, out_shape=(pltpu.VMEM((256, 128), BF), pltpu.VMEM(...  78.6 us
    pallas_call x1, Pallas kernels, local(): pl.pallas_call(finish, out_shape=(shape((16, D), BF), shape((8, 16), F32)...  4.08 us

profile of v5, /device:TPU:1, one launch (start us, length us, event | category | flops | bytes accessed | tf_op | source)
XLA Modules:
  0.0 83.5 jit_solution(4943524214575580360)
XLA Ops:
  0.6 0.0 copy-start
  0.6 0.0 copy-start.1
  0.7 0.0 copy-start.2
  0.7 78.6 %moe_grad.1 = (bf16[256,128]{1,0:T(8,128)(2,1)S(1)}, bf16[256,1152]{1,0:T(8,128)(2,1)S(1)}, bf16[16,3712]{1,0:T(8,128)(2,1)S(1)}, bf16[3,3584,128]{2,1,0:T(8,128...) custom-call(bf16[16,3584]{1,0:T(8,128)(2,1)} %tok.1, bf16[16,3584]{1,0:T(8,128)(2,1)} %ups.1, ...), custom_call_target="tpu_custom_call" | custom-call | tf_op jit(solution)/shard_map/moe_grad/pallas_call | solution.py:507
  79.3 0.0 copy-done
  79.3 0.0 copy-done.1
  79.3 0.0 copy-done.2
  79.3 4.1 %moe_finish.1 = (bf16[16,3584]{1,0:T(8,128)(2,1)}, f32[8,16]{1,0:T(8,128)}, bf16[3,3584,128]{2,1,0:T(8,128)(2,1)}, bf16[3,3584,128]{2,1,0:T(8,128)(2,1)}, bf16[3,128,3584]{2,1,0:T(8,128)(2,1)}) custom-call(bf16[256,128]{1,0:T(8,128)(2,1)S(1)} %get-tuple-element.16.amat, bf16[256,1152]{1,0:T(8,128)(2,1)S(1)} %get-tuple-element.17.got_b, ...), custom_call_target="tpu_custom_call" | custom-call | tf_op jit(solution)/shard_map/moe_finish/pallas_call | solution.py:550
Async XLA Ops:
  0.6 78.6 %copy-start = (s32[16,8]{0,1:T(8,128)S(1)}, s32[16,8]{0,1:T(8,128)}, u32[]{:S(2)}) copy-start(s32[16,8]{0,1:T(8,128)} %param.11) | copy-start | bytes 1540
  0.6 78.6 %copy-start.1 = (f32[256]{0:T(256)S(1)}, f32[256]{0:T(256)}, u32[]{:S(2)}) copy-start(f32[256]{0:T(256)} %param.14) | copy-start | bytes 3076
  0.7 78.6 %copy-start.2 = (s32[16]{0:T(128)S(1)}, s32[16]{0:T(128)}, u32[]{:S(2)}) copy-start(s32[16]{0:T(128)} %param.13) | copy-start | bytes 196

commit v6 on v5

--- a/solution.py
+++ b/solution.py
@@ -327,9 +327,8 @@
         pb[rows, pl.ds(D, 128)] = score.astype(BF)
 
         def partial(first, last):
-            @pl.loop(first, last)
-            def _(i):
-                cols = pl.ds(pl.multiple_of(i * 512, 512), 512)
+            for i in range(first, last):
+                cols = pl.ds(512 * i, 512)
                 pb[rows, cols] = lax.dot_general(
                     dall[rows, :], wall[cols, :], NT, preferred_element_type=F32
                 ).astype(BF)

time: 83.7 us -> 81.4 us (0.973)
  Pallas kernels: 82.7 us -> 80.4 us
    pallas_call x1, Pallas kernels: 78.6 us -> 76.3 us  [local(): pl.pallas_call(kernel, out_shape=(pltpu.VMEM((256, 128), BF), pltpu.VMEM(...]
where the time goes in v6:
time: 81.4 us; the launch traced here: 81.3 us
  Pallas kernels  80.4 us (99%)
  between operations  0.85 us (1%)
    pallas_call x1, Pallas kernels, local(): pl.pallas_call(kernel, out_shape=(pltpu.VMEM((256, 128), BF), pltpu.VMEM(...  76.3 us
    pallas_call x1, Pallas kernels, local(): pl.pallas_call(finish, out_shape=(shape((16, D), BF), shape((8, 16), F32)...  4.08 us

profile of v6, /device:TPU:1, one launch (start us, length us, event | category | flops | bytes accessed | tf_op | source)
XLA Modules:
  0.0 81.3 jit_solution(11223168031052205070)
XLA Ops:
  0.6 0.0 copy-start
  0.6 0.0 copy-start.1
  0.7 0.0 copy-start.2
  0.7 76.3 %moe_grad.1 = (bf16[256,128]{1,0:T(8,128)(2,1)S(1)}, bf16[256,1152]{1,0:T(8,128)(2,1)S(1)}, bf16[16,3712]{1,0:T(8,128)(2,1)S(1)}, bf16[3,3584,128]{2,1,0:T(8,128...) custom-call(bf16[16,3584]{1,0:T(8,128)(2,1)} %tok.1, bf16[16,3584]{1,0:T(8,128)(2,1)} %ups.1, ...), custom_call_target="tpu_custom_call" | custom-call | tf_op jit(solution)/shard_map/moe_grad/pallas_call | solution.py:506
  77.0 0.0 copy-done
  77.0 0.0 copy-done.1
  77.0 0.0 copy-done.2
  77.0 4.1 %moe_finish.1 = (bf16[16,3584]{1,0:T(8,128)(2,1)}, f32[8,16]{1,0:T(8,128)}, bf16[3,3584,128]{2,1,0:T(8,128)(2,1)}, bf16[3,3584,128]{2,1,0:T(8,128)(2,1)}, bf16[3,128,3584]{2,1,0:T(8,128)(2,1)}) custom-call(bf16[256,128]{1,0:T(8,128)(2,1)S(1)} %get-tuple-element.16.amat, bf16[256,1152]{1,0:T(8,128)(2,1)S(1)} %get-tuple-element.17.got_b, ...), custom_call_target="tpu_custom_call" | custom-call | tf_op jit(solution)/shard_map/moe_finish/pallas_call | solution.py:549
Async XLA Ops:
  0.6 76.4 %copy-start = (s32[16,8]{0,1:T(8,128)S(1)}, s32[16,8]{0,1:T(8,128)}, u32[]{:S(2)}) copy-start(s32[16,8]{0,1:T(8,128)} %param.11) | copy-start | bytes 1540
  0.6 76.4 %copy-start.1 = (f32[256]{0:T(256)S(1)}, f32[256]{0:T(256)}, u32[]{:S(2)}) copy-start(f32[256]{0:T(256)} %param.14) | copy-start | bytes 3076
  0.7 76.4 %copy-start.2 = (s32[16]{0:T(128)S(1)}, s32[16]{0:T(128)}, u32[]{:S(2)}) copy-start(s32[16]{0:T(128)} %param.13) | copy-start | bytes 196
